TPU v7x, 256 devices: a whole 4x4x8 slice. The times are simulated.
256 devices in a mesh: row: 16 (over y, x_hi, core), col: 16 (over x_lo, z).
Axes of the slice: x: 4 (x_hi: 2, x_lo: 2; x = x_hi * 2 + x_lo), y: 4, z: 8, core: 2. Of those that a mesh axis runs over, the one named last changes fastest.
Arguments:
- features: bfloat16 [16, 4096, 256], P('col', 'row'), may hold values from -6 to 6
- tile_values: bfloat16 [16, 16, 160, 128, 128], P('row', 'col'), may hold values from 0 to 0.17675781
- tile_rows: int32 [16, 16, 160], P('row', 'col'), may hold values from 0 to 31
- tile_cols: int32 [16, 16, 160], P('row', 'col'), may hold values from 0 to 31
- tile_counts: int32 [16, 16], P('row', 'col'), may hold values from 40 to 160, as said below
- weight: bfloat16 [256, 256], replicated, may hold values from -0.375 to 0.375
- cotangent: bfloat16 [16, 4096, 256], P('row', 'col'), may hold values from -6 to 6
Outputs:
- activated: bfloat16 [16, 4096, 256], P('row', 'col')
- weight_grad: float32 [256, 256], replicated
- feature_grad: bfloat16 [16, 4096, 256], P('col', 'row')
Inputs may be any that keep to these rules, and one draw needn't show every extreme that they name: `tile_counts`: in every draw some grid block has exactly 160 live slots.
All inputs are finite; a program needn't handle non-finite values.
Results may differ from a plain program's by a relative error of at most 0.04.
Values may be sent and summed in bfloat16 or wider, within the bound.
No kernel may reach another device: no remote copies, remote signals or barrier semaphores. Data moves between devices by JAX's collectives and lax.ppermute only.
A program may use at most 128 MiB of HBM per device.

v0:
```python
import jax
import jax.numpy as jnp
from jax import lax
from jax.sharding import PartitionSpec as P


def body(features, tile_values, tile_rows, tile_cols, tile_counts, weight, cotangent):
    node_rows = features.shape[1]
    feature_width = features.shape[2]
    tile_size = tile_values.shape[-1]
    slot_count = tile_values.shape[2]
    row_tiles = lax.axis_size("col") * node_rows // tile_size
    col_tiles = lax.axis_size("row") * node_rows // tile_size
    total_nodes = node_rows * lax.axis_size("row") * lax.axis_size("col")
    row_index = tile_rows.reshape(slot_count)
    col_index = tile_cols.reshape(slot_count)
    live_slots = jnp.arange(slot_count) < tile_counts.reshape(())
    values = jnp.where(
        live_slots[:, None, None],
        tile_values.reshape(slot_count, tile_size, tile_size),
        jnp.zeros((), jnp.bfloat16),
    )
    row_indicator = (row_index[None, :] == jnp.arange(row_tiles)[:, None]).astype(jnp.float32)
    column_indicator = (col_index[None, :] == jnp.arange(col_tiles)[:, None]).astype(jnp.float32)
    contract_rows = (((0,), (0,)), ((), ()))
    contract_cols = (((1,), (1,)), ((), ()))
    gathered = lax.all_gather(features, "row", axis=1, tiled=True)
    picked = gathered.reshape(col_tiles, tile_size, feature_width)[col_index]
    products = jnp.einsum("tab,tbf->taf", values, picked, preferred_element_type=jnp.float32)
    partial_rows = jnp.einsum("rt,taf->raf", row_indicator, products, precision=lax.Precision.HIGH)
    partial_rows = partial_rows.reshape(row_tiles * tile_size, feature_width)
    own_sums = lax.psum_scatter(
        partial_rows.astype(jnp.bfloat16), "col", scatter_dimension=0, tiled=True
    )
    pre = jnp.dot(own_sums, weight, preferred_element_type=jnp.float32)
    sigmoid_pre = jax.nn.sigmoid(pre)
    slope = sigmoid_pre * (1.0 + pre * (1.0 - sigmoid_pre))
    upstream = (cotangent.reshape(node_rows, feature_width).astype(jnp.float32) * slope).astype(
        jnp.bfloat16
    )
    downstream_rows = lax.dot_general(
        upstream, weight, contract_cols, preferred_element_type=jnp.float32
    ).astype(jnp.bfloat16)
    down_full = lax.all_gather(downstream_rows, "col", axis=0, tiled=True)
    activated = (pre * sigmoid_pre).astype(jnp.bfloat16)
    weight_portion = lax.dot_general(
        own_sums, upstream, contract_rows, preferred_element_type=jnp.float32
    )
    weight_grad = lax.psum(weight_portion, ("row", "col")) * float(total_nodes) ** (-0.5)
    picked_back = down_full.reshape(row_tiles, tile_size, feature_width)[row_index]
    backward_products = jnp.einsum(
        "tab,taf->tbf", values, picked_back, preferred_element_type=jnp.float32
    )
    column_terms = jnp.einsum(
        "xu,uhv->xhv", column_indicator, backward_products, precision=lax.Precision.HIGH
    )
    column_terms = column_terms.reshape(col_tiles * tile_size, feature_width)
    feature_grad = lax.psum_scatter(
        column_terms.astype(jnp.bfloat16), "row", scatter_dimension=0, tiled=True
    )
    return (
        activated.reshape(1, node_rows, feature_width),
        weight_grad,
        feature_grad.reshape(1, node_rows, feature_width),
    )


def solution(mesh):
    in_specs = (
        P("col", "row", None),
        P("row", "col", None, None, None),
        P("row", "col", None),
        P("row", "col", None),
        P("row", "col"),
        P(),
        P("row", "col", None),
    )
    out_specs = (P("row", "col", None), P(), P("col", "row", None))
    return jax.shard_map(body, mesh=mesh, in_specs=in_specs, out_specs=out_specs, check_vma=False)
```

profile of v0, /device:TPU:1, one launch (start us, length us, event | category | flops | bytes accessed | tf_op | source)
XLA Modules:
  0.0 600.1 jit_solution(3997221212887183523)
XLA Ops:
  7.2 0.0 copy-start
  7.2 0.0 all-gather.3.cloned.1.call-start
  7.2 0.7 all-gather.3.cloned.1.call-update
  7.9 0.0 reduce-scatter.3.cloned.1.call-start
  8.6 0.7 compare_select_fusion.1
  9.3 58.3 %all-gather.3.cloned.1.call-done = bf16[1,4096,256]{2,1,0:T(8,128)(2,1)} async-done(((bf16[1,256,256]{2,1,0:T(8,128)(2,1)}), bf16[1,4096,256]{2,1,0:T(8,128)(2,1)}) %all-gather.3.cloned.1.call-update) | async-done | bytes 2097168 | tf_op jit(solution)/shard_map/all_gather | solution.py:27
  67.6 9.2 %gather_fusion = bf16[160,128,256]{2,1,0:T(8,128)(2,1)} fusion(bf16[32,128,256]{2,1,0:T(8,128)(2,1)} %bitcast.39, s32[1024]{0:T(1024)S(1)} %pad_clamp_fusion.1), kind=kCustom, calls=%fused_computation | custom fusion | bytes 20972160 | tf_op jit(solution)/shard_map/gather | solution.py:28
  76.8 15.5 %fusion.5 = f32[160,128,256]{2,1,0:T(8,128)} fusion(bf16[160,128,256]{2,1,0:T(8,128)(2,1)} %gather_fusion, bf16[1,1,160,128,128]{4,3,2,1,0:T(8,128)(2,1)} %param.8, pred[160]{0:T(512)(128)(4,1)S(1)} %iota_compare_fusion.2), kind=kOutput, calls=%fused_computation.8 | convolution fusion | flops 1344798720 | bytes 36700320 | tf_op jit(solution)/shard_map/tab,tbf->taf/dot_general | solution.py:29
  92.3 0.0 copy-done.1
  92.3 21.4 %fusion.6 = bf16[32,128,256]{2,0,1:T(8,128)(2,1)S(1)} fusion(f32[160,128,256]{2,1,0:T(8,128)} %fusion.5, s32[160]{0:T(256)S(1)} %bitcast.42), kind=kOutput, calls=%fused_computation.9 | convolution fusion | flops 1007686656 | bytes 23069312 | tf_op jit(solution)/shard_map/rt,taf->raf/dot_general | solution.py:30
  113.7 2.5 copy.10
  116.2 0.0 reduce-scatter.3.cloned.1.call-update
  116.2 0.0 all-gather.5.cloned.1.call-start
  116.3 61.5 %reduce-scatter.3.cloned.1.call-done = bf16[256,256]{1,0:T(8,128)(2,1)} async-done(((bf16[4096,256]{1,0:T(8,128)(2,1)}), bf16[256,256]{1,0:T(8,128)(2,1)}) %reduce-scatter.3.cloned.1.call-update) | async-done | bytes 131088 | tf_op jit(solution)/shard_map/reduce_scatter | solution.py:32
  177.8 0.0 copy-done
  177.8 1.8 fusion.12
  179.6 0.9 convolution_convert_fusion
  180.5 0.0 all-gather.5.cloned.1.call-update
  180.5 0.0 all-reduce.2.cloned.1.call-start
  180.6 1.8 fusion.22
  182.4 0.0 all-reduce.2.cloned.1.call-update
  182.4 0.0 reduce-scatter.5.cloned.1.call-start
  182.5 67.5 %all-gather.5.cloned.1.call-done = bf16[4096,256]{1,0:T(8,128)(2,1)} async-done(((bf16[256,256]{1,0:T(8,128)(2,1)}), bf16[4096,256]{1,0:T(8,128)(2,1)}) %all-gather.5.cloned.1.call-update) | async-done | bytes 2097168 | tf_op jit(solution)/shard_map/all_gather | solution.py:44
  250.0 9.4 %gather_fusion.1 = bf16[160,128,256]{2,1,0:T(8,128)(2,1)} fusion(bf16[32,128,256]{2,1,0:T(8,128)(2,1)} %bitcast.38, s32[1024]{0:T(1024)S(1)} %pad_clamp_fusion), kind=kCustom, calls=%fused_computation.1 | custom fusion | bytes 20972160 | tf_op jit(solution)/shard_map/gather | solution.py:50
  259.4 0.0 copy-start.2
  259.4 16.2 %fusion.4 = f32[160,128,256]{2,1,0:T(8,128)} fusion(bf16[160,128,256]{2,1,0:T(8,128)(2,1)} %gather_fusion.1, bf16[1,1,160,128,128]{4,3,2,1,0:T(8,128)(2,1)} %param.8, pred[160]{0:T(512)(128)(4,1)S(1)} %iota_compare_fusion.2), kind=kOutput, calls=%fused_computation.7 | convolution fusion | flops 1344798720 | bytes 36700320 | tf_op jit(solution)/shard_map/tab,taf->tbf/dot_general | solution.py:51
  275.7 21.5 %fusion.9 = bf16[32,128,256]{2,0,1:T(8,128)(2,1)S(1)} fusion(f32[160,128,256]{2,1,0:T(8,128)} %fusion.4, s32[160]{0:T(256)S(1)} %bitcast.43), kind=kOutput, calls=%fused_computation.10 | convolution fusion | flops 1007686656 | bytes 23069312 | tf_op jit(solution)/shard_map/xu,uhv->xhv/dot_general | solution.py:54
  297.2 2.5 copy.11
  299.7 0.0 reduce-scatter.5.cloned.1.call-update
  299.7 212.0 %all-reduce.2.cloned.1.call-done = f32[256,256]{1,0:T(8,128)} async-done(((f32[256,256]{1,0:T(8,128)}), f32[256,256]{1,0:T(8,128)}) %all-reduce.2.cloned.1.call-update) | async-done | bytes 262160 | tf_op jit(solution)/shard_map/psum | solution.py:49
  511.7 1.7 broadcast_multiply_fusion
  513.3 79.8 %reduce-scatter.5.cloned.1.call-done = bf16[256,256]{1,0:T(8,128)(2,1)} async-done(((bf16[4096,256]{1,0:T(8,128)(2,1)}), bf16[256,256]{1,0:T(8,128)(2,1)}) %reduce-scatter.5.cloned.1.call-update) | async-done | bytes 131088 | tf_op jit(solution)/shard_map/reduce_scatter | solution.py:58
  (8 shorter events, 0.0 us)
Async XLA Ops:
  7.2 170.6 %copy-start = (bf16[256,256]{1,0:T(8,128)(2,1)S(1)}, bf16[256,256]{1,0:T(8,128)(2,1)}, u32[]{:S(2)}) copy-start(bf16[256,256]{1,0:T(8,128)(2,1)} %param.12) | copy-start | bytes 393220
  7.2 60.4 %all-gather.3.cloned.1.call-start = ((), (), s32[]{:S(2)}) async-start(), calls=%async_computation.2 | async-start | bytes 2228224 | tf_op jit(solution)/shard_map/all_gather | solution.py:27
  7.9 169.8 %reduce-scatter.3.cloned.1.call-start = ((), (), s32[]{:S(2)}) async-start(), calls=%async_computation.3 | async-start | bytes 2228224 | tf_op jit(solution)/shard_map/reduce_scatter | solution.py:32
  76.8 15.5 %copy-start.1 = (s32[1,1,160]{2,1,0:T(1,128)S(1)}, s32[1,1,160]{2,1,0:T(1,128)}, u32[]{:S(2)}) copy-start(s32[1,1,160]{2,1,0:T(1,128)} %param.9) | copy-start | bytes 1924
  92.3 85.5 %copy-start.3 = (bf16[1,256,256]{2,1,0:T(8,128)(2,1)S(1)}, bf16[1,256,256]{2,1,0:T(8,128)(2,1)}, u32[]{:S(2)}) copy-start(bf16[1,256,256]{2,1,0:T(8,128)(2,1)} %param.13) | copy-start | bytes 393220
  116.2 133.8 %all-gather.5.cloned.1.call-start = ((), (), s32[]{:S(2)}) async-start(), calls=%async_computation.5 | async-start | bytes 2228224 | tf_op jit(solution)/shard_map/all_gather | solution.py:44
  180.5 331.2 %all-reduce.2.cloned.1.call-start = ((), (), s32[]{:S(2)}) async-start(), calls=%async_computation.4 | async-start | bytes 524288 | tf_op jit(solution)/shard_map/psum | solution.py:49
  182.4 410.7 %reduce-scatter.5.cloned.1.call-start = ((), (), s32[]{:S(2)}) async-start(), calls=%async_computation.6 | async-start | bytes 2228224 | tf_op jit(solution)/shard_map/reduce_scatter | solution.py:58
  259.4 16.3 %copy-start.2 = (s32[1,1,160]{2,1,0:T(1,128)S(1)}, s32[1,1,160]{2,1,0:T(1,128)}, u32[]{:S(2)}) copy-start(s32[1,1,160]{2,1,0:T(1,128)} %param.10) | copy-start | bytes 1924
Sparse Core Ops, SparseCore 0:
  10.8 56.7 all-gather.2
  116.4 61.3 reduce-scatter.2
  180.6 69.3 all-gather.4
  255.9 255.7 all-reduce.1
  516.3 76.8 reduce-scatter.4
where the time goes:
time: 611 us; the launch traced here: 600 us
  waiting for transfers between devices  480 us (79%)
  matrix products  79.1 us (13%)
  local copies, waits for them, and re-layouts  23.7 us (4%)
  between operations  14.9 us (2%)
    psum x1, waiting for transfers between devices, body(): lax.psum(weight_portion, ('row', 'col')) * float(total_nodes) ** (-0.5)  212 us
    reduce_scatter x1, waiting for transfers between devices, body(): lax.psum_scatter(column_terms.astype(jnp.bfloat16), 'row', scatter_dimens...  79.8 us
    all_gather x1, waiting for transfers between devices, body(): down_full = lax.all_gather(downstream_rows, 'col', axis=0, tiled=True)  67.5 us
    reduce_scatter x1, waiting for transfers between devices, body(): lax.psum_scatter(partial_rows.astype(jnp.bfloat16), 'col', scatter_dimens...  61.5 us
    all_gather x1, waiting for transfers between devices, body(): gathered = lax.all_gather(features, 'row', axis=1, tiled=True)  58.3 us
    dot_general x1, matrix products, body(): jnp.einsum('xu,uhv->xhv', column_indicator, backward_products, precision=...  21.5 us
    dot_general x1, matrix products, body(): jnp.einsum('rt,taf->raf', row_indicator, products, precision=lax.Precisio...  21.4 us
    dot_general x1, matrix products, body(): jnp.einsum('tab,taf->tbf', values, picked_back, preferred_element_type=jn...  16.2 us
  transfers between devices with their start and end apart: 5, of which 5 were waited for; matrix products, arithmetic and copies ran while one was open for 9% of the time, Pallas kernels for 0%

commit v1 on v0

v1 whole, which is shorter than its diff:
```python
import functools

import jax
import jax.numpy as jnp
from jax import lax
from jax.experimental import pallas as pl
from jax.experimental.pallas import tpu as pltpu
from jax.sharding import PartitionSpec as P

GROUP = 16
VMEM = pl.BlockSpec(memory_space=pltpu.VMEM)
SMEM = pl.BlockSpec(memory_space=pltpu.SMEM)


def params(mib):
    return pltpu.CompilerParams(vmem_limit_bytes=mib * 2**20)


def spmm_kernel(transposed, pieces, live, dst, src, *refs):
    sources, (tiles, *outs, held, total) = refs[:pieces], refs[pieces:]
    tile = tiles.shape[-1]
    at = 0
    for piece in sources:
        held[at : at + piece.shape[0], :] = piece[...]
        at += piece.shape[0]
    total[...] = jnp.zeros_like(total)
    count = live[0]
    contract = (((0 if transposed else 1,), (0,)), ((), ()))

    def step(group, carry):
        products = []
        for unit in range(GROUP):
            slot = group * GROUP + unit
            rows = pl.ds(pl.multiple_of(src[slot] * tile, tile), tile)
            values = tiles[slot]
            values = jnp.where(slot < count, values, jnp.zeros_like(values))
            products.append(
                lax.dot_general(values, held[rows, :], contract, preferred_element_type=jnp.float32)
            )
        for unit in range(GROUP):
            rows = pl.ds(pl.multiple_of(dst[group * GROUP + unit] * tile, tile), tile)
            total[rows, :] += products[unit]
        return carry

    lax.fori_loop(0, (count + GROUP - 1) // GROUP, step, 0)
    at = 0
    for out in outs:
        out[...] = total[at : at + out.shape[0], :].astype(out.dtype)
        at += out.shape[0]


def spmm(transposed, live, dst, src, sources, tiles, parts):
    slots, tile, _ = tiles.shape
    width = sources[0].shape[1]
    depth = sum(piece.shape[0] for piece in sources)
    flops = 2 * slots * tile * tile * width
    out = pl.pallas_call(
        functools.partial(spmm_kernel, transposed, len(sources)),
        out_shape=[jax.ShapeDtypeStruct((depth // parts, width), jnp.bfloat16)] * parts,
        in_specs=[SMEM] * 3 + [VMEM] * (len(sources) + 1),
        out_specs=[VMEM] * parts,
        scratch_shapes=[
            pltpu.VMEM((depth, width), jnp.bfloat16),
            pltpu.VMEM((depth, width), jnp.float32),
        ],
        compiler_params=params(40),
        cost_estimate=pl.CostEstimate(
            flops=flops, bytes_accessed=9 * 2**20, transcendentals=0
        ),
        name="spmm_back" if transposed else "spmm",
    )(live, dst, src, *sources, tiles)
    return out


def dense_kernel(received, weight, cotangent, activated, down, weight_terms):
    sums = received[0].astype(jnp.float32)
    for part in range(1, received.shape[0]):
        sums += received[part].astype(jnp.float32)
    aggregated = sums.astype(jnp.bfloat16)
    pre = jnp.dot(aggregated, weight[...], preferred_element_type=jnp.float32)
    gate = jax.nn.sigmoid(pre)
    activated[...] = (pre * gate).astype(jnp.bfloat16)
    slope = gate * (1.0 + pre * (1.0 - gate))
    upstream = (cotangent[...].astype(jnp.float32) * slope).astype(jnp.bfloat16)
    down[...] = lax.dot_general(
        upstream, weight[...], (((1,), (1,)), ((), ())), preferred_element_type=jnp.float32
    ).astype(jnp.bfloat16)
    weight_terms[...] = lax.dot_general(
        aggregated, upstream, (((0,), (0,)), ((), ())), preferred_element_type=jnp.float32
    )


def dense(received, weight, cotangent):
    rows, width = cotangent.shape
    return pl.pallas_call(
        dense_kernel,
        out_shape=[
            jax.ShapeDtypeStruct((rows, width), jnp.bfloat16),
            jax.ShapeDtypeStruct((rows, width), jnp.bfloat16),
            jax.ShapeDtypeStruct((width, width), jnp.float32),
        ],
        in_specs=[VMEM] * 3,
        out_specs=[VMEM] * 3,
        compiler_params=params(24),
        name="dense",
    )(received, weight, cotangent)


def body(features, tile_values, tile_rows, tile_cols, tile_counts, weight, cotangent):
    node_rows, width = features.shape[1:]
    slots, tile = tile_values.shape[2:4]
    rows_n, cols_n = lax.axis_size("row"), lax.axis_size("col")
    chips = rows_n // 2
    core = lax.axis_index("row") % 2
    same_core = [[2 * k + c for k in range(chips)] for c in range(2)]
    swap = [(i, i ^ 1) for i in range(rows_n)]
    live = tile_counts.reshape(1)
    tiles = tile_values.reshape(slots, tile, tile)
    row_tiles = tile_rows.reshape(slots)
    per = node_rows // tile
    owner, inner = tile_cols.reshape(slots) // per, tile_cols.reshape(slots) % per
    col_tiles = ((((owner % 2) ^ core) * chips) + owner // 2) * per + inner

    own = lax.all_to_all(
        jnp.broadcast_to(features, (chips, node_rows, width)), "row", 0, 0,
        axis_index_groups=same_core, tiled=True,
    ).reshape(chips * node_rows, width)
    other = lax.ppermute(own, "row", swap)
    (block,) = spmm(False, live, row_tiles, col_tiles, [own, other], tiles, 1)
    received = lax.all_to_all(block.reshape(cols_n, node_rows, width), "col", 0, 0, tiled=True)
    activated, down, terms = dense(received, weight, cotangent.reshape(node_rows, width))

    down_all = lax.all_to_all(
        jnp.broadcast_to(down[None], (cols_n, node_rows, width)), "col", 0, 0, tiled=True
    ).reshape(cols_n * node_rows, width)

    share = lax.all_to_all(terms.reshape(rows_n, -1, width), "row", 0, 0, tiled=True)
    share = jnp.sum(share, axis=0)
    share = lax.all_to_all(share.reshape(cols_n, -1, width), "col", 0, 0, tiled=True)
    share = jnp.sum(share, axis=0) * float(node_rows * rows_n * cols_n) ** (-0.5)
    share = lax.all_to_all(
        jnp.broadcast_to(share[None], (cols_n, *share.shape)), "col", 0, 0, tiled=True
    ).reshape(-1, width)
    weight_grad = lax.all_to_all(
        jnp.broadcast_to(share[None], (rows_n, *share.shape)), "row", 0, 0, tiled=True
    ).reshape(width, width)

    mine, theirs = spmm(True, live, col_tiles, row_tiles, [down_all], tiles, 2)
    swapped = lax.ppermute(theirs, "row", swap)
    pair = (mine.astype(jnp.float32) + swapped.astype(jnp.float32)).astype(jnp.bfloat16)
    back = lax.all_to_all(
        pair.reshape(chips, node_rows, width), "row", 0, 0,
        axis_index_groups=same_core, tiled=True,
    )
    feature_grad = jnp.sum(back.astype(jnp.float32), axis=0).astype(jnp.bfloat16)
    return (
        activated.reshape(1, node_rows, width),
        weight_grad,
        feature_grad.reshape(1, node_rows, width),
    )


def solution(mesh):
    in_specs = (
        P("col", "row", None),
        P("row", "col", None, None, None),
        P("row", "col", None),
        P("row", "col", None),
        P("row", "col"),
        P(),
        P("row", "col", None),
    )
    out_specs = (P("row", "col", None), P(), P("col", "row", None))
    return jax.shard_map(body, mesh=mesh, in_specs=in_specs, out_specs=out_specs, check_vma=False)
```

time: 611 us -> 227 us (0.37); the launches traced: 600 us -> 227 us
  waiting for transfers between devices: 480 us -> 24.9 us
  blocking collectives: 0 us -> 170 us
  matrix products: 79.1 us -> 0 us
  local copies, waits for them, and re-layouts: 23.7 us -> 5.15 us
  starting transfers between devices: 0.2 us -> 16.5 us
  between operations: 14.9 us -> 1.38 us
  Pallas kernels: 0 us -> 7.17 us
    psum x1 -> x0, waiting for transfers between devices: 212 us -> none  [body(): lax.psum(weight_portion, ('row', 'col')) * float(total_nodes) ** (-0.5)]
    all_to_all x0 -> x6, blocking collectives: none -> 170 us  [the longest x1 59.7 us: body(): lax.all_to_all(block.reshape(cols_n, node_rows, width), 'col', 0, 0, tile...]
    reduce_scatter x2 -> x0, waiting for transfers between devices: 141 us -> none  [the longest x1 79.8 us: body(): lax.psum_scatter(column_terms.astype(jnp.bfloat16), 'row', scatter_dimens...]
    all_gather x2 -> x0, waiting for transfers between devices: 126 us -> none  [the longest x1 67.5 us: body(): down_full = lax.all_gather(downstream_rows, 'col', axis=0, tiled=True)]
    dot_general x7 -> x0, matrix products: 79.1 us -> none  [the longest x1 21.5 us: body(): jnp.einsum('xu,uhv->xhv', column_indicator, backward_products, precision=...]
    all_to_all x0 -> x2, waiting for transfers between devices: none -> 23.3 us  [the longest x1 15.9 us: body(): lax.all_to_all(pair.reshape(chips, node_rows, width), 'row', 0, 0, axis_i...]
    gather x2 -> x0, local copies, waits for them, and re-layouts: 18.6 us -> none  [the longest x1 9.38 us: body(): down_full.reshape(row_tiles, tile_size, feature_width)[row_index]]
    all_to_all x0 -> x2, starting transfers between devices: none -> 10.4 us  [the longest x1 6.87 us: body(): lax.all_to_all(jnp.broadcast_to(share[None], (rows_n, *share.shape)), 'ro...]
  transfers between devices with their start and end apart: 5 -> 4, of which waited for: 5 -> 3; matrix products, arithmetic and copies ran while one was open for 9% -> 1% of each run, Pallas kernels for 0% -> 0%
where the time goes in v1:
time: 227 us
  blocking collectives  170 us (75%)
  waiting for transfers between devices  24.9 us (11%)
  starting transfers between devices  16.5 us (7%)
  Pallas kernels  7.17 us (3%)
  local copies, waits for them, and re-layouts  5.15 us (2%)
    all_to_all x1, blocking collectives, body(): lax.all_to_all(block.reshape(cols_n, node_rows, width), 'col', 0, 0, tile...  59.7 us
    all_to_all x1, blocking collectives, body(): lax.all_to_all(jnp.broadcast_to(down[None], (cols_n, node_rows, width)),...  51.6 us
    all_to_all x1, blocking collectives, body(): lax.all_to_all(jnp.broadcast_to(features, (chips, node_rows, width)), 'ro...  23.6 us
    all_to_all x1, waiting for transfers between devices, body(): lax.all_to_all(pair.reshape(chips, node_rows, width), 'row', 0, 0, axis_i...  15.9 us
    all_to_all x1, blocking collectives, body(): lax.all_to_all(share.reshape(cols_n, -1, width), 'col', 0, 0, tiled=True)  12.7 us
    all_to_all x1, blocking collectives, body(): lax.all_to_all(terms.reshape(rows_n, -1, width), 'row', 0, 0, tiled=True)  12.2 us
    all_to_all x1, blocking collectives, body(): lax.all_to_all(jnp.broadcast_to(share[None], (cols_n, *share.shape)), 'co...  9.89 us
    all_to_all x1, waiting for transfers between devices, body(): lax.all_to_all(jnp.broadcast_to(share[None], (rows_n, *share.shape)), 'ro...  7.46 us
  transfers between devices with their start and end apart: 4, of which 3 were waited for; matrix products, arithmetic and copies ran while one was open for 1% of the time, Pallas kernels for 0%

profile of v1, /device:TPU:1, one launch (start us, length us, event | category | flops | bytes accessed | tf_op | source)
XLA Modules:
  0.0 227.0 jit_solution(15154700640139230170)
XLA Ops:
  0.6 0.0 copy-start.4
  0.6 0.0 copy-start.3
  0.7 1.0 broadcast_in_dim.13
  1.6 23.6 %all_to_all.40 = bf16[8,256,256]{2,1,0:T(8,128)(2,1)S(1)} all-to-all(bf16[8,256,256]{2,1,0:T(8,128)(2,1)S(1)} %broadcast_in_dim.13), channel_id=1, replica_groups={{0,32,64,96,128,160,192,224},{16,48,80,112,144,176,208,240},{1,33,65,97..., dimensions={0} | all-to-all | bytes 2097152 | tf_op jit(solution)/shard_map/all_to_all | solution.py:124
  25.2 1.9 collective-permute-start
  27.7 0.0 copy-done.4
  27.8 1.6 collective-permute-done.refs_1_
  29.4 0.0 copy-done.3
  29.4 2.5 %copy-done = bf16[1,1,160,128,128]{4,3,2,1,0:T(8,128)(2,1)S(1)} copy-done((bf16[1,1,160,128,128]{4,3,2,1,0:T(8,128)(2,1)S(1)}, bf16[1,1,160,128,128]{4,3,2,1,0:T(8,128)(2,1)}, u32[]{:S(2)}) %copy-start) | copy-done | bytes 5242904
  31.9 2.9 %spmm.1 = bf16[4096,256]{1,0:T(8,128)(2,1)S(1)} custom-call(s32[1]{0:T(128)} %bitcast.17.live, s32[160]{0:T(256)S(1)} %bitcast.29, s32[160]{0:T(256)S(1)} %fusion.2.src.dst, bf16[2048,256]{1,0:T(8,128)(2,1)S(1)} %bitcast.26, bf16[2048,256]{1,0:T(8,128)(2,1)S(1)} %collective-permute-done.refs_1_, bf16[160,128,128]{2,1,0:T(8,128)(2,1)S(1)} %bitcast.19), custom_call_target="tpu_custom_call" | custom-call | flops 1342177280 | bytes 9437184 | tf_op jit(solution)/shard_map/spmm/pallas_call | solution.py:57
  34.8 0.0 slice-start
  34.8 59.7 %all_to_all.41.received = bf16[16,256,256]{2,1,0:T(8,128)(2,1)S(1)} all-to-all(bf16[16,256,256]{2,1,0:T(8,128)(2,1)S(1)} %bitcast.24), channel_id=1, replica_groups=mesh['row'=16,'col'=16] {'col'}, dimensions={0} | all-to-all | bytes 4194304 | tf_op jit(solution)/shard_map/all_to_all | solution.py:130
  94.5 0.0 copy-done.1
  94.5 0.0 copy-done.2
  94.5 1.1 dense.1
  95.6 0.2 broadcast_in_dim.31
  95.8 51.6 %all_to_all.42 = bf16[16,256,256]{2,1,0:T(8,128)(2,1)S(1)} all-to-all(bf16[16,256,256]{2,1,0:T(8,128)(2,1)S(1)} %broadcast_in_dim.31), channel_id=1, replica_groups=mesh['row'=16,'col'=16] {'col'}, dimensions={0} | all-to-all | bytes 4194304 | tf_op jit(solution)/shard_map/all_to_all | solution.py:133
  147.4 0.0 slice-done
  147.4 3.2 %spmm_back.1 = (bf16[2048,256]{1,0:T(8,128)(2,1)S(1)}, bf16[2048,256]{1,0:T(8,128)(2,1)S(1)}) custom-call(s32[1]{0:T(128)} %bitcast.18.live, s32[160]{0:T(256)S(1)} %fusion.2.src.dst, s32[160]{0:T(256)S(1)} %bitcast.30, bf16[4096,256]{1,0:T(8,128)(2,1)S(1)} %bitcast.23, bf16[160,128,128]{2,1,0:T(8,128)(2,1)S(1)} %bitcast.22), custom_call_target="tpu_custom_call" | custom-call | flops 1342177280 | bytes 9437184 | tf_op jit(solution)/shard_map/spmm_back/pallas_call | solution.py:57
  150.6 4.2 %collective-permute-start.1 = (bf16[2048,256]{1,0:T(8,128)(2,1)S(1)}, bf16[2048,256]{1,0:T(8,128)(2,1)S(1)}, u32[]{:S(2)}, u32[]{:S(2)}) collective-permute-start(bf16[2048,256]{1,0:T(8,128)(2,1)S(1)} %get-tuple-element.12), channel_id=1, source_target_pairs={{0,16},{16,0},{32,48},{48,32},{64,80},{80,64},{96,112},{112,96},{1... | collective-permute-start | bytes 3145736 | tf_op jit(solution)/shard_map/ppermute | solution.py:149
  154.8 12.2 %all_to_all.43 = f32[16,16,256]{2,1,0:T(8,128)S(1)} all-to-all(f32[16,16,256]{2,1,0:T(8,128)S(1)} %bitcast.27), channel_id=1, replica_groups=mesh['row'=16,'col'=16] {'row'}, dimensions={0} | all-to-all | bytes 524288 | tf_op jit(solution)/shard_map/all_to_all | solution.py:137
  167.0 12.7 %all_to_all.44 = f32[16,1,256]{2,1,0:T(1,128)S(1)} all-to-all(f32[16,1,256]{2,1,0:T(1,128)S(1)} %reshape.69), channel_id=1, replica_groups=mesh['row'=16,'col'=16] {'col'}, dimensions={0} | all-to-all | bytes 32768 | tf_op jit(solution)/shard_map/all_to_all | solution.py:139
  179.8 9.9 %all_to_all.45 = f32[16,1,256]{2,1,0:T(1,128)S(1)} all-to-all(f32[16,1,256]{2,1,0:T(1,128)S(1)} %broadcast_in_dim.28), channel_id=1, replica_groups=mesh['row'=16,'col'=16] {'col'}, dimensions={0} | all-to-all | bytes 32768 | tf_op jit(solution)/shard_map/all_to_all | solution.py:141
  189.7 0.7 broadcast_in_dim.30
  190.5 6.9 %all-to-all-start.5 = ((f32[16,16,256]{2,1,0:T(8,128)}), f32[16,16,256]{2,1,0:T(8,128)S(1)}, u32[]{:S(2)}, u32[]{:S(2)}) async-start(f32[16,16,256]{2,1,0:T(8,128)} %broadcast_in_dim.30), calls=%async_computation.5 | async-start | bytes 524288 | tf_op jit(solution)/shard_map/all_to_all | solution.py:144
  197.3 0.0 collective-permute-done.1
  197.3 1.3 add_convert_fusion
  198.6 7.5 %all-to-all-done.5 = f32[16,16,256]{2,1,0:T(8,128)S(1)} async-done(((f32[16,16,256]{2,1,0:T(8,128)}), f32[16,16,256]{2,1,0:T(8,128)S(1)}, u32[]{:S(2)}, u32[]{:S(2)}) %all-to-all-start.5) | async-done | bytes 262176 | tf_op jit(solution)/shard_map/all_to_all | solution.py:144
  206.1 3.6 %all-to-all-start.7 = ((bf16[8,256,256]{2,1,0:T(8,128)(2,1)}), bf16[8,256,256]{2,1,0:T(8,128)(2,1)S(1)}, u32[]{:S(2)}, u32[]{:S(2)}) async-start(bf16[8,256,256]{2,1,0:T(8,128)(2,1)} %bitcast.12), calls=%async_computation.7 | async-start | bytes 2097152 | tf_op jit(solution)/shard_map/all_to_all | solution.py:151
  209.6 15.9 %all-to-all-done.7 = bf16[8,256,256]{2,1,0:T(8,128)(2,1)S(1)} async-done(((bf16[8,256,256]{2,1,0:T(8,128)(2,1)}), bf16[8,256,256]{2,1,0:T(8,128)(2,1)S(1)}, u32[]{:S(2)}, u32[]{:S(2)}) %all-to-all-start.7) | async-done | bytes 1048608 | tf_op jit(solution)/shard_map/all_to_all | solution.py:151
  225.5 0.8 reduce_sum.32
  226.3 0.7 copy.15
  (13 shorter events, 0.1 us)
Async XLA Ops:
  0.6 27.1 %copy-start.4 = (s32[1,1,160]{2,1,0:T(1,128)S(1)}, s32[1,1,160]{2,1,0:T(1,128)}, u32[]{:S(2)}) copy-start(s32[1,1,160]{2,1,0:T(1,128)} %param.10) | copy-start | bytes 1924
  0.6 28.7 %copy-start.3 = (s32[1,1,160]{2,1,0:T(1,128)S(1)}, s32[1,1,160]{2,1,0:T(1,128)}, u32[]{:S(2)}) copy-start(s32[1,1,160]{2,1,0:T(1,128)} %param.9) | copy-start | bytes 1924
  25.2 4.2 %collective-permute-start = (bf16[2048,256]{1,0:T(8,128)(2,1)S(1)}, bf16[2048,256]{1,0:T(8,128)(2,1)S(1)}, u32[]{:S(2)}, u32[]{:S(2)}) collective-permute-start(bf16[2048,256]{1,0:T(8,128)(2,1)S(1)} %bitcast.25), channel_id=1, source_target_pairs={{0,16},{16,0},{32,48},{48,32},{64,80},{80,64},{96,112},{112,96},{1... | collective-permute-start | bytes 3145736 | tf_op jit(solution)/shard_map/ppermute | solution.py:128
  29.4 2.5 %copy-start = (bf16[1,1,160,128,128]{4,3,2,1,0:T(8,128)(2,1)S(1)}, bf16[1,1,160,128,128]{4,3,2,1,0:T(8,128)(2,1)}, u32[]{:S(2)}) copy-start(bf16[1,1,160,128,128]{4,3,2,1,0:T(8,128)(2,1)} %param.8) | copy-start | bytes 15728644
  31.9 62.6 %copy-start.1 = (bf16[256,256]{1,0:T(8,128)(2,1)S(1)}, bf16[256,256]{1,0:T(8,128)(2,1)}, u32[]{:S(2)}) copy-start(bf16[256,256]{1,0:T(8,128)(2,1)} %weight.1) | copy-start | bytes 393220
  31.9 62.6 %copy-start.2 = (bf16[1,256,256]{2,1,0:T(8,128)(2,1)S(1)}, bf16[1,256,256]{2,1,0:T(8,128)(2,1)}, u32[]{:S(2)}) copy-start(bf16[1,256,256]{2,1,0:T(8,128)(2,1)} %param.13) | copy-start | bytes 393220
  34.8 112.6 %slice-start = ((s8[5242880]{0:T(1024)(128)(4,1)}), s8[4194304]{0:T(1024)(128)(4,1)S(1)}, s32[]{:S(2)}) async-start(s8[5242880]{0:T(1024)(128)(4,1)} %bitcast.20), calls=%async_computation.8 | async-start | bytes 8388608
  94.5 52.9 %slice-start.1 = ((s8[5242880]{0:T(1024)(128)(4,1)}), s8[1048576]{0:T(1024)(128)(4,1)S(1)}, s32[]{:S(2)}) async-start(s8[5242880]{0:T(1024)(128)(4,1)} %bitcast.20), calls=%async_computation.9 | async-start | bytes 2097152
  150.6 46.7 %collective-permute-start.1 = (bf16[2048,256]{1,0:T(8,128)(2,1)S(1)}, bf16[2048,256]{1,0:T(8,128)(2,1)S(1)}, u32[]{:S(2)}, u32[]{:S(2)}) collective-permute-start(bf16[2048,256]{1,0:T(8,128)(2,1)S(1)} %get-tuple-element.12), channel_id=1, source_target_pairs={{0,16},{16,0},{32,48},{48,32},{64,80},{80,64},{96,112},{112,96},{1... | collective-permute-start | bytes 3145736 | tf_op jit(solution)/shard_map/ppermute | solution.py:149
  190.5 15.6 %all-to-all-start.5 = ((f32[16,16,256]{2,1,0:T(8,128)}), f32[16,16,256]{2,1,0:T(8,128)S(1)}, u32[]{:S(2)}, u32[]{:S(2)}) async-start(f32[16,16,256]{2,1,0:T(8,128)} %broadcast_in_dim.30), calls=%async_computation.5 | async-start | bytes 524288 | tf_op jit(solution)/shard_map/all_to_all | solution.py:144
  206.1 19.4 %all-to-all-start.7 = ((bf16[8,256,256]{2,1,0:T(8,128)(2,1)}), bf16[8,256,256]{2,1,0:T(8,128)(2,1)S(1)}, u32[]{:S(2)}, u32[]{:S(2)}) async-start(bf16[8,256,256]{2,1,0:T(8,128)(2,1)} %bitcast.12), calls=%async_computation.7 | async-start | bytes 2097152 | tf_op jit(solution)/shard_map/all_to_all | solution.py:151

commit v2 on v1

v2 whole, which is shorter than its diff:
```python
import functools

import jax
import jax.numpy as jnp
from jax import lax
from jax.experimental import pallas as pl
from jax.experimental.pallas import tpu as pltpu
from jax.sharding import PartitionSpec as P

GROUP = 32
VMEM = pl.BlockSpec(memory_space=pltpu.VMEM)
SMEM = pl.BlockSpec(memory_space=pltpu.SMEM)
HBM = pl.BlockSpec(memory_space=pltpu.HBM)
DMA = pltpu.SemaphoreType.DMA


def params(mib):
    return pltpu.CompilerParams(vmem_limit_bytes=mib * 2**20)


def shape(dtype, *dims):
    return jax.ShapeDtypeStruct(dims, dtype)


def f32(ref):
    return ref[...].astype(jnp.float32)


def copy_all(pairs, sems):
    copies = [pltpu.make_async_copy(a, b, sems.at[i]) for i, (a, b) in enumerate(pairs)]
    for copy in copies:
        copy.start()
    for copy in copies:
        copy.wait()


def spread_kernel(source, out, sems):
    copy_all([(source, out.at[i]) for i in range(out.shape[0])], sems)


def spread(source, copies):
    return pl.pallas_call(
        spread_kernel,
        out_shape=shape(source.dtype, copies, *source.shape),
        in_specs=[VMEM],
        out_specs=HBM,
        scratch_shapes=[DMA((copies,))],
        compiler_params=params(4),
        name="spread",
    )(source)


def spmm_kernel(transposed, pieces, live, dst, src, *refs):
    sources, tiles = refs[: len(pieces)], refs[len(pieces)]
    outs = refs[len(pieces) + 1 : -4]
    held, total, buffer, sems = refs[-4:]
    tile = tiles.shape[-1]
    count = live[0]
    groups = (count + GROUP - 1) // GROUP

    def load(group):
        slots = pl.ds(group * GROUP, GROUP)
        return pltpu.make_async_copy(tiles.at[slots], buffer.at[slots], sems.at[group])

    def begin(group, carry):
        load(group).start()
        return carry

    lax.fori_loop(0, groups, begin, 0)
    at = 0
    for rows, piece in zip(pieces, sources):
        held[at : at + rows, :] = piece[:rows, :]
        at += rows
    total[...] = jnp.zeros_like(total)
    contract = (((0 if transposed else 1,), (0,)), ((), ()))

    def step(group, carry):
        load(group).wait()
        products = []
        for unit in range(GROUP):
            slot = group * GROUP + unit
            rows = pl.ds(pl.multiple_of(src[slot] * tile, tile), tile)
            values = buffer[slot]
            values = jnp.where(slot < count, values, jnp.zeros_like(values))
            products.append(
                lax.dot_general(values, held[rows, :], contract, preferred_element_type=jnp.float32)
            )
        for unit in range(GROUP):
            rows = pl.ds(pl.multiple_of(dst[group * GROUP + unit] * tile, tile), tile)
            total[rows, :] += products[unit]
        return carry

    lax.fori_loop(0, groups, step, 0)
    at = 0
    for out in outs:
        out[...] = total[at : at + out.shape[0], :].astype(out.dtype)
        at += out.shape[0]


def spmm(transposed, live, dst, src, sources, pieces, tiles, parts):
    slots, tile, _ = tiles.shape
    width = sources[0].shape[1]
    depth = sum(pieces)
    return pl.pallas_call(
        functools.partial(spmm_kernel, transposed, pieces),
        out_shape=[shape(jnp.bfloat16, rows, width) for rows in parts],
        in_specs=[SMEM] * 3 + [VMEM] * len(sources) + [HBM],
        out_specs=[VMEM] * len(parts),
        scratch_shapes=[
            pltpu.VMEM((depth, width), jnp.bfloat16),
            pltpu.VMEM((depth, width), jnp.float32),
            pltpu.VMEM(tiles.shape, tiles.dtype),
            DMA((slots // GROUP,)),
        ],
        compiler_params=params(20),
        cost_estimate=pl.CostEstimate(
            flops=20 * slots * tile * tile * width, bytes_accessed=36 * 2**20, transcendentals=0
        ),
        name="spmm_back" if transposed else "spmm",
    )(live, dst, src, *sources, pltpu.with_memory_space_constraint(tiles, pltpu.HBM))


def add_at_kernel(start, first, second, out):
    end = start + second.shape[0]
    out[start:end, :] = (first[start:end, :].astype(jnp.float32) + f32(second)).astype(out.dtype)
    if start > 0:
        out[:start, :] = first[:start, :]
    if end < out.shape[0]:
        out[end:, :] = first[end:, :]


def add_at(first, second, start=0):
    return pl.pallas_call(
        functools.partial(add_at_kernel, start),
        out_shape=shape(first.dtype, *first.shape),
        in_specs=[VMEM] * 2,
        out_specs=VMEM,
        compiler_params=params(6),
        name="add_at",
    )(first, second)


def part_sum(parts):
    sums = parts[0].astype(jnp.float32)
    for part in range(1, parts.shape[0]):
        sums += parts[part].astype(jnp.float32)
    return sums


def split_sum_kernel(own, first, second, mine, theirs):
    sums = f32(own) + f32(first) + f32(second)
    mine[...] = sums[: mine.shape[0]]
    theirs[...] = sums[mine.shape[0] :].astype(theirs.dtype)


def split_sum(own, first, second):
    rows, width = own.shape
    return pl.pallas_call(
        split_sum_kernel,
        out_shape=[shape(jnp.float32, rows // 2, width), shape(own.dtype, rows // 2, width)],
        in_specs=[VMEM] * 3,
        out_specs=[VMEM] * 2,
        compiler_params=params(4),
        name="split_sum",
    )(own, first, second)


def whole_sum_kernel(parts, out):
    out[...] = part_sum(parts).astype(out.dtype)


def whole_sum(parts):
    return pl.pallas_call(
        whole_sum_kernel,
        out_shape=shape(parts.dtype, *parts.shape[1:]),
        in_specs=[VMEM],
        out_specs=VMEM,
        compiler_params=params(6),
        name="whole_sum",
    )(parts)


def dense_kernel(mine, swapped, weight, cotangent, activated, sent):
    rows = cotangent.shape[0]
    aggregated = (mine[...] + f32(swapped)).astype(jnp.bfloat16)
    pre = jnp.dot(aggregated, weight[...], preferred_element_type=jnp.float32)
    gate = jax.nn.sigmoid(pre)
    slope = gate * (1.0 + pre * (1.0 - gate))
    upstream = (cotangent[...].astype(jnp.float32) * slope).astype(jnp.bfloat16)
    sent[:rows, :] = lax.dot_general(
        upstream, weight[...], (((1,), (1,)), ((), ())), preferred_element_type=jnp.float32
    ).astype(jnp.bfloat16)
    sent[rows:, :] = lax.dot_general(
        aggregated, upstream, (((0,), (0,)), ((), ())), preferred_element_type=jnp.float32
    ).astype(jnp.bfloat16)
    activated[...] = (pre * gate).astype(jnp.bfloat16)


def dense(mine, swapped, weight, cotangent):
    rows, width = cotangent.shape
    return pl.pallas_call(
        dense_kernel,
        out_shape=[
            shape(jnp.bfloat16, rows, width),
            shape(jnp.bfloat16, rows + width, width),
        ],
        in_specs=[VMEM] * 4,
        out_specs=[VMEM] * 2,
        compiler_params=params(12),
        name="dense",
    )(mine, swapped, weight, cotangent)


def begin_kernel(place, sent, received, pair, rising, sums):
    rows = pair.shape[0] // 2
    along, part = sums.shape[:2]
    for out in (pair, rising):
        out[:rows, :] = sent[:rows, :]
        out[rows : 2 * rows, :] = received[:rows, :]
    for i in range(along):
        at = slice(rows + i * part, rows + (i + 1) * part)
        sums[i] = sent[at, :].astype(jnp.float32) + received[at, :].astype(jnp.float32)
    far = lax.rem(place[0] + along // 2, along)
    rising[2 * rows :, :] = sums[far].astype(rising.dtype)


def begin(place, sent, received, rows, along):
    width = sent.shape[1]
    part = (sent.shape[0] - rows) // along
    return pl.pallas_call(
        begin_kernel,
        out_shape=[
            shape(sent.dtype, 2 * rows, width),
            shape(sent.dtype, 2 * rows + part, width),
            shape(jnp.float32, along, part, width),
        ],
        in_specs=[SMEM] + [VMEM] * 2,
        out_specs=[VMEM] * 3,
        compiler_params=params(8),
        name="begin",
    )(place, sent, received)


def pass_on_kernel(first, last, offset, held, place, arrived, sums, out):
    rows = last - first
    along, part = sums.shape[:2]
    out[:rows, :] = arrived[first:last, :]
    term = sums[lax.rem(place[0] + offset, along)]
    if arrived.shape[0] > held:
        term += arrived[held:, :].astype(jnp.float32)
    out[rows:, :] = term.astype(out.dtype)


def pass_on(first, last, offset, held, place, arrived, sums):
    _, part, width = sums.shape
    return pl.pallas_call(
        functools.partial(pass_on_kernel, first, last, offset, held),
        out_shape=shape(arrived.dtype, last - first + part, width),
        in_specs=[SMEM] + [VMEM] * 2,
        out_specs=VMEM,
        compiler_params=params(6),
        name="pass_on",
    )(place, arrived, sums)


def ring_sum_kernel(place, rising, falling, sums, out, stage, sems):
    part = sums.shape[1]
    total = sums[place[0]]
    total += rising[rising.shape[0] - part :, :].astype(jnp.float32)
    total += falling[falling.shape[0] - part :, :].astype(jnp.float32)
    stage[...] = total.astype(stage.dtype)
    copy_all([(stage, out.at[i]) for i in range(out.shape[0])], sems)


def ring_sum(place, rising, falling, sums, copies):
    _, part, width = sums.shape
    return pl.pallas_call(
        ring_sum_kernel,
        out_shape=shape(rising.dtype, copies, part, width),
        in_specs=[SMEM] + [VMEM] * 3,
        out_specs=HBM,
        scratch_shapes=[pltpu.VMEM((part, width), rising.dtype), DMA((copies,))],
        compiler_params=params(4),
        name="ring_sum",
    )(place, rising, falling, sums)


def scaled_sum_kernel(scale, parts, out):
    out[...] = part_sum(parts) * scale


def scaled_sum(parts, scale):
    return pl.pallas_call(
        functools.partial(scaled_sum_kernel, scale),
        out_shape=shape(jnp.float32, *parts.shape[1:]),
        in_specs=[VMEM],
        out_specs=VMEM,
        compiler_params=params(4),
        name="scaled_sum",
    )(parts)


def arrange_kernel(place, *refs):
    pieces, out = refs[:-1], refs[-1]
    part = pieces[0].shape[0]
    for turn, piece in enumerate(pieces):
        at = lax.rem(place[0] + turn, len(pieces))
        out[pl.ds(pl.multiple_of(at * part, part), part), :] = piece[...]


def arrange(place, pieces):
    part, width = pieces[0].shape
    return pl.pallas_call(
        arrange_kernel,
        out_shape=shape(pieces[0].dtype, part * len(pieces), width),
        in_specs=[SMEM] + [VMEM] * len(pieces),
        out_specs=VMEM,
        compiler_params=params(4),
        name="arrange",
    )(place, *pieces)


def body(features, tile_values, tile_rows, tile_cols, tile_counts, weight, cotangent):
    node_rows, width = features.shape[1:]
    slots, tile = tile_values.shape[2:4]
    rows_n, cols_n = lax.axis_size("row"), lax.axis_size("col")
    chips, along = rows_n // 2, cols_n // 2
    core, side = lax.axis_index("row") % 2, lax.axis_index("col") // along
    place = lax.axis_index("col") % along
    same_core = [[2 * k + c for k in range(chips)] for c in range(2)]
    core_swap = [(i, i ^ 1) for i in range(rows_n)]
    side_swap = [(i, (i + along) % cols_n) for i in range(cols_n)]
    up = [(i, i - i % along + (i + 1) % along) for i in range(cols_n)]
    back = [(j, i) for i, j in up]
    live = tile_counts.reshape(1)
    tiles = tile_values.reshape(slots, tile, tile)
    per = node_rows // tile

    col_owner, col_inner = tile_cols.reshape(slots) // per, tile_cols.reshape(slots) % per
    by_core = ((((col_owner % 2) ^ core) * chips) + col_owner // 2) * per + col_inner
    row_owner, row_inner = tile_rows.reshape(slots) // per, tile_rows.reshape(slots) % per
    far = along // 2
    distance = (row_owner % along - place + along) % along
    nearest = jnp.where(
        distance < far, 2 * distance, jnp.where(distance == far, along - 1, 2 * (along - distance) - 1)
    )
    farthest = jnp.where(
        distance == 0, along - 1,
        jnp.where(distance <= far, along - 1 - 2 * distance + (distance == far), 2 * distance - along),
    )
    within = ((row_owner // along) ^ side) * per + row_inner
    by_nearest, by_farthest = nearest * 2 * per + within, farthest * 2 * per + within

    def exchange(x, axis, groups=None):
        return lax.all_to_all(x, axis, 0, 0, axis_index_groups=groups, tiled=True)

    def flat(x):
        return x.reshape(-1, x.shape[-1])

    own = flat(exchange(spread(features.reshape(node_rows, width), chips), "row", same_core))
    other = lax.ppermute(own, "row", core_swap)
    pair = 2 * node_rows
    blocks = spmm(
        False, live, by_farthest, by_core, [own, other], [chips * node_rows] * 2, tiles,
        [node_rows] * 2 + [pair] * (along - 1),
    )
    rising, falling = blocks[0], blocks[1]
    for step in range(1, far):
        rising = lax.ppermute(rising, "col", up)
        falling = lax.ppermute(falling, "col", back)
        rising = add_at(blocks[2 * step], rising)
        falling = add_at(blocks[2 * step + 1], falling, pair - falling.shape[0])
    rising = lax.ppermute(rising, "col", up)
    falling = lax.ppermute(falling, "col", back)
    mine, theirs = split_sum(blocks[-1], rising, falling)
    swapped = lax.ppermute(theirs, "col", side_swap)
    spot = place.reshape(1)
    activated, sent = dense(mine, swapped, weight, cotangent.reshape(node_rows, width))

    received = lax.ppermute(sent, "col", side_swap)
    both, rising, sums = begin(spot, sent, received, node_rows, along)
    falling = both
    sources = [both]
    for step in range(1, far):
        rising = lax.ppermute(rising, "col", up)
        falling = lax.ppermute(falling, "col", back)
        sources += [rising, falling]
        cut = node_rows if step == far - 1 else 0
        rising = pass_on(0, pair - cut, far - step, pair, spot, rising, sums)
        falling = pass_on(cut, pair, far + step, pair, spot, falling, sums)
    rising = lax.ppermute(rising, "col", up)
    falling = lax.ppermute(falling, "col", back)
    sources += [rising, falling]
    terms = ring_sum(spot, rising, falling, sums, rows_n)
    terms, *sources = lax.optimization_barrier((terms, *sources))
    terms = exchange(terms, "row")

    mine, theirs = spmm(
        True, live, by_core, by_nearest, sources, [pair] * (along - 1) + [node_rows] * 2,
        tiles, [chips * node_rows] * 2,
    )
    scale = float(node_rows * rows_n * cols_n) ** (-0.5)
    own_share = scaled_sum(terms, scale)
    own_share, mine, theirs = lax.optimization_barrier((own_share, mine, theirs))
    shares = add_at(mine, lax.ppermute(theirs, "row", core_swap))
    shares = exchange(shares.reshape(chips, node_rows, width), "row", same_core)
    feature_grad = whole_sum(shares)

    turned = [
        lax.ppermute(
            own_share, "col", [(i, i - i % along + (i - turn) % along) for i in range(cols_n)]
        )
        for turn in range(1, along)
    ]
    weight_grad = arrange(spot, [own_share] + turned)
    return (
        activated.reshape(1, node_rows, width),
        weight_grad,
        feature_grad.reshape(1, node_rows, width),
    )


def solution(mesh):
    in_specs = (
        P("col", "row", None),
        P("row", "col", None, None, None),
        P("row", "col", None),
        P("row", "col", None),
        P("row", "col"),
        P(),
        P("row", "col", None),
    )
    out_specs = (P("row", "col", None), P(), P("col", "row", None))
    return jax.shard_map(body, mesh=mesh, in_specs=in_specs, out_specs=out_specs, check_vma=False)
```

time: 227 us -> 165 us (0.73)
  blocking collectives: 170 us -> 23.6 us
  starting transfers between devices: 16.5 us -> 63 us
  waiting for transfers between devices: 24.9 us -> 55.9 us
  Pallas kernels: 7.17 us -> 18 us
  local copies, waits for them, and re-layouts: 5.15 us -> 1.89 us
    all_to_all x6 -> x1, blocking collectives: 170 us -> 23.6 us  [exchange(): return lax.all_to_all(x, axis, 0, 0, axis_index_groups=groups, tiled=True)]
    ppermute x2 -> x27, waiting for transfers between devices: 1.6 us -> 51.9 us  [the longest x8 32.2 us: body(): falling = lax.ppermute(falling, 'col', back)]
    ppermute x2 -> x27, starting transfers between devices: 6.1 us -> 45 us  [the longest x8 28.2 us: body(): falling = lax.ppermute(falling, 'col', back)]
    all_to_all x2, waiting for transfers between devices: 23.3 us -> 3.93 us  [exchange(): return lax.all_to_all(x, axis, 0, 0, axis_index_groups=groups, tiled=True)]
    pallas_call x3 -> x23, Pallas kernels: 7.17 us -> 18 us  [the longest x2 11.5 us: spmm(): pl.pallas_call(functools.partial(spmm_kernel, transposed, pieces), out_sh...]
    all_to_all x2, starting transfers between devices: 10.4 us -> 18 us  [exchange(): return lax.all_to_all(x, axis, 0, 0, axis_index_groups=groups, tiled=True)]
  transfers between devices with their start and end apart: 4 -> 29, of which waited for: 3 -> 19; matrix products, arithmetic and copies ran while one was open for 1% -> 1% of each run, Pallas kernels for 0% -> 4%
where the time goes in v2:
time: 165 us
  starting transfers between devices  63 us (38%)
  waiting for transfers between devices  55.9 us (34%)
  blocking collectives  23.6 us (14%)
  Pallas kernels  18 us (11%)
  local copies, waits for them, and re-layouts  1.89 us (1%)
    ppermute x8, waiting for transfers between devices, body(): falling = lax.ppermute(falling, 'col', back)  32.2 us
    ppermute x8, starting transfers between devices, body(): falling = lax.ppermute(falling, 'col', back)  28.2 us
    all_to_all x1, blocking collectives, exchange(): return lax.all_to_all(x, axis, 0, 0, axis_index_groups=groups, tiled=True)  23.6 us
    all_to_all x2, starting transfers between devices, exchange(): return lax.all_to_all(x, axis, 0, 0, axis_index_groups=groups, tiled=True)  18 us
    pallas_call x2, Pallas kernels, spmm(): pl.pallas_call(functools.partial(spmm_kernel, transposed, pieces), out_sh...  11.5 us
    ppermute x7, starting transfers between devices, body(): lax.ppermute(own_share, 'col', [(i, i - i % along + (i - turn) % along) f...  10.1 us
    ppermute x8, waiting for transfers between devices, body(): rising = lax.ppermute(rising, 'col', up)  6.48 us
    ppermute x1, waiting for transfers between devices, body(): received = lax.ppermute(sent, 'col', side_swap)  4.52 us
  transfers between devices with their start and end apart: 29, of which 19 were waited for; matrix products, arithmetic and copies ran while one was open for 1% of the time, Pallas kernels for 4%

profile of v2, /device:TPU:1, one launch (start us, length us, event | category | flops | bytes accessed | tf_op | source)
XLA Modules:
  0.0 165.2 jit_solution(9868602210868348367)
XLA Ops:
  2.9 23.6 %all_to_all.15 = bf16[8,256,256]{2,1,0:T(8,128)(2,1)S(1)} all-to-all(bf16[8,256,256]{2,1,0:T(8,128)(2,1)S(1)} %spread.1), channel_id=1, replica_groups={{0,32,64,96,128,160,192,224},{16,48,80,112,144,176,208,240},{1,33,65,97..., dimensions={0} | all-to-all | bytes 2097152 | tf_op jit(solution)/shard_map/all_to_all | solution.py:355
  26.5 1.9 %collective-permute-start = (bf16[2048,256]{1,0:T(8,128)(2,1)S(1)}, bf16[2048,256]{1,0:T(8,128)(2,1)S(1)}, u32[]{:S(2)}, u32[]{:S(2)}) collective-permute-start(bf16[2048,256]{1,0:T(8,128)(2,1)S(1)} %bitcast.13), channel_id=1, source_target_pairs={{0,16},{16,0},{32,48},{48,32},{64,80},{80,64},{96,112},{112,96},{1... | collective-permute-start | bytes 3145736 | tf_op jit(solution)/shard_map/ppermute | solution.py:361
  30.7 5.6 %spmm.1 = (bf16[256,256]{1,0:T(8,128)(2,1)S(1)}, bf16[256,256]{1,0:T(8,128)(2,1)S(1)}, bf16[512,256]{1,0:T(8,128)(2,1)S(1)}, bf16[512,256]{1,0:T(8,128)(2,1)S(1)...) custom-call(s32[1]{0:T(128)} %bitcast.11.live, ...), custom_call_target="tpu_custom_call" | custom-call | flops 13421772800 | bytes 37748736 | tf_op jit(solution)/shard_map/spmm/pallas_call | solution.py:104
  36.3 4.9 %collective-permute-start.5 = (bf16[256,256]{1,0:T(8,128)(2,1)S(1)}, bf16[256,256]{1,0:T(8,128)(2,1)S(1)}, u32[]{:S(2)}, u32[]{:S(2)}) collective-permute-start(bf16[256,256]{1,0:T(8,128)(2,1)S(1)} %get-tuple-element.42), channel_id=1, source_target_pairs={{1,0},{2,1},{3,2},{4,3},{5,4},{6,5},{7,6},{0,7},{9,8},{10,9},{11,1... | collective-permute-start | bytes 393224 | tf_op jit(solution)/shard_map/ppermute | solution.py:370
  41.3 3.2 %collective-permute-done.5.second = bf16[256,256]{1,0:T(8,128)(2,1)S(1)} collective-permute-done((bf16[256,256]{1,0:T(8,128)(2,1)S(1)}, bf16[256,256]{1,0:T(8,128)(2,1)S(1)}, u32[]{:S(2)}, u32[]{:S(2)}) %collective-permute-start.5) | collective-permute-done | bytes 131104 | tf_op jit(solution)/shard_map/ppermute | solution.py:370
  44.5 3.5 %collective-permute-start.6 = (bf16[512,256]{1,0:T(8,128)(2,1)S(1)}, bf16[512,256]{1,0:T(8,128)(2,1)S(1)}, u32[]{:S(2)}, u32[]{:S(2)}) collective-permute-start(bf16[512,256]{1,0:T(8,128)(2,1)S(1)} %add_at.10), channel_id=1, source_target_pairs={{1,0},{2,1},{3,2},{4,3},{5,4},{6,5},{7,6},{0,7},{9,8},{10,9},{11,1... | collective-permute-start | bytes 786440 | tf_op jit(solution)/shard_map/ppermute | solution.py:370
  48.1 5.0 %collective-permute-done.6.second = bf16[512,256]{1,0:T(8,128)(2,1)S(1)} collective-permute-done((bf16[512,256]{1,0:T(8,128)(2,1)S(1)}, bf16[512,256]{1,0:T(8,128)(2,1)S(1)}, u32[]{:S(2)}, u32[]{:S(2)}) %collective-permute-start.6) | collective-permute-done | bytes 262176 | tf_op jit(solution)/shard_map/ppermute | solution.py:370
  53.2 3.5 %collective-permute-start.7 = (bf16[512,256]{1,0:T(8,128)(2,1)S(1)}, bf16[512,256]{1,0:T(8,128)(2,1)S(1)}, u32[]{:S(2)}, u32[]{:S(2)}) collective-permute-start(bf16[512,256]{1,0:T(8,128)(2,1)S(1)} %add_at.11), channel_id=1, source_target_pairs={{1,0},{2,1},{3,2},{4,3},{5,4},{6,5},{7,6},{0,7},{9,8},{10,9},{11,1... | collective-permute-start | bytes 786440 | tf_op jit(solution)/shard_map/ppermute | solution.py:370
  56.8 4.1 %collective-permute-done.7.second = bf16[512,256]{1,0:T(8,128)(2,1)S(1)} collective-permute-done((bf16[512,256]{1,0:T(8,128)(2,1)S(1)}, bf16[512,256]{1,0:T(8,128)(2,1)S(1)}, u32[]{:S(2)}, u32[]{:S(2)}) %collective-permute-start.7) | collective-permute-done | bytes 262176 | tf_op jit(solution)/shard_map/ppermute | solution.py:370
  61.0 3.5 %collective-permute-start.8 = (bf16[512,256]{1,0:T(8,128)(2,1)S(1)}, bf16[512,256]{1,0:T(8,128)(2,1)S(1)}, u32[]{:S(2)}, u32[]{:S(2)}) collective-permute-start(bf16[512,256]{1,0:T(8,128)(2,1)S(1)} %add_at.12), channel_id=1, source_target_pairs={{1,0},{2,1},{3,2},{4,3},{5,4},{6,5},{7,6},{0,7},{9,8},{10,9},{11,1... | collective-permute-start | bytes 786440 | tf_op jit(solution)/shard_map/ppermute | solution.py:374
  64.6 3.2 %collective-permute-done.8.second = bf16[512,256]{1,0:T(8,128)(2,1)S(1)} collective-permute-done((bf16[512,256]{1,0:T(8,128)(2,1)S(1)}, bf16[512,256]{1,0:T(8,128)(2,1)S(1)}, u32[]{:S(2)}, u32[]{:S(2)}) %collective-permute-start.8) | collective-permute-done | bytes 262176 | tf_op jit(solution)/shard_map/ppermute | solution.py:374
  67.8 3.3 %collective-permute-done.4.first = bf16[512,256]{1,0:T(8,128)(2,1)S(1)} collective-permute-done((bf16[512,256]{1,0:T(8,128)(2,1)S(1)}, bf16[512,256]{1,0:T(8,128)(2,1)S(1)}, u32[]{:S(2)}, u32[]{:S(2)}) %collective-permute-start.4) | collective-permute-done | bytes 262176 | tf_op jit(solution)/shard_map/ppermute | solution.py:373
  72.8 2.4 %collective-permute-done.9.swapped = bf16[256,256]{1,0:T(8,128)(2,1)S(1)} collective-permute-done((bf16[256,256]{1,0:T(8,128)(2,1)S(1)}, bf16[256,256]{1,0:T(8,128)(2,1)S(1)}, u32[]{:S(2)}, u32[]{:S(2)}) %collective-permute-start.9) | collective-permute-done | bytes 131104 | tf_op jit(solution)/shard_map/ppermute | solution.py:376
  77.5 4.5 %collective-permute-done.10.received = bf16[512,256]{1,0:T(8,128)(2,1)S(1)} collective-permute-done((bf16[512,256]{1,0:T(8,128)(2,1)S(1)}, bf16[512,256]{1,0:T(8,128)(2,1)S(1)}, u32[]{:S(2)}, u32[]{:S(2)}) %collective-permute-start.10) | collective-permute-done | bytes 262176 | tf_op jit(solution)/shard_map/ppermute | solution.py:380
  82.2 2.7 %collective-permute-start.15 = (bf16[512,256]{1,0:T(8,128)(2,1)S(1)}, bf16[512,256]{1,0:T(8,128)(2,1)S(1)}, u32[]{:S(2)}, u32[]{:S(2)}) collective-permute-start(bf16[512,256]{1,0:T(8,128)(2,1)S(1)} %get-tuple-element.51.refs_0_), channel_id=1, source_target_pairs={{1,0},{2,1},{3,2},{4,3},{5,4},{6,5},{7,6},{0,7},{9,8},{10,9},{11,1... | collective-permute-start | bytes 786440 | tf_op jit(solution)/shard_map/ppermute | solution.py:386
  84.8 3.3 %collective-permute-done.15.arrived.refs_2_ = bf16[512,256]{1,0:T(8,128)(2,1)S(1)} collective-permute-done((bf16[512,256]{1,0:T(8,128)(2,1)S(1)}, bf16[512,256]{1,0:T(8,128)(2,1)S(1)}, u32[]{:S(2)}, u32[]{:S(2)}) %collective-permute-start.15) | collective-permute-done | bytes 262176 | tf_op jit(solution)/shard_map/ppermute | solution.py:386
  88.2 3.4 %collective-permute-start.16 = (bf16[544,256]{1,0:T(8,128)(2,1)S(1)}, bf16[544,256]{1,0:T(8,128)(2,1)S(1)}, u32[]{:S(2)}, u32[]{:S(2)}) collective-permute-start(bf16[544,256]{1,0:T(8,128)(2,1)S(1)} %pass_on.9), channel_id=1, source_target_pairs={{1,0},{2,1},{3,2},{4,3},{5,4},{6,5},{7,6},{0,7},{9,8},{10,9},{11,1... | collective-permute-start | bytes 835592 | tf_op jit(solution)/shard_map/ppermute | solution.py:386
  91.7 6.2 %collective-permute-done.16.arrived.refs_4_ = bf16[544,256]{1,0:T(8,128)(2,1)S(1)} collective-permute-done((bf16[544,256]{1,0:T(8,128)(2,1)S(1)}, bf16[544,256]{1,0:T(8,128)(2,1)S(1)}, u32[]{:S(2)}, u32[]{:S(2)}) %collective-permute-start.16) | collective-permute-done | bytes 278560 | tf_op jit(solution)/shard_map/ppermute | solution.py:386
  97.9 3.3 %collective-permute-start.17 = (bf16[544,256]{1,0:T(8,128)(2,1)S(1)}, bf16[544,256]{1,0:T(8,128)(2,1)S(1)}, u32[]{:S(2)}, u32[]{:S(2)}) collective-permute-start(bf16[544,256]{1,0:T(8,128)(2,1)S(1)} %pass_on.10), channel_id=1, source_target_pairs={{1,0},{2,1},{3,2},{4,3},{5,4},{6,5},{7,6},{0,7},{9,8},{10,9},{11,1... | collective-permute-start | bytes 835592 | tf_op jit(solution)/shard_map/ppermute | solution.py:386
  101.3 5.3 %collective-permute-done.17.arrived.refs_6_ = bf16[544,256]{1,0:T(8,128)(2,1)S(1)} collective-permute-done((bf16[544,256]{1,0:T(8,128)(2,1)S(1)}, bf16[544,256]{1,0:T(8,128)(2,1)S(1)}, u32[]{:S(2)}, u32[]{:S(2)}) %collective-permute-start.17) | collective-permute-done | bytes 278560 | tf_op jit(solution)/shard_map/ppermute | solution.py:386
  106.6 3.5 %collective-permute-start.18 = (bf16[288,256]{1,0:T(8,128)(2,1)S(1)}, bf16[288,256]{1,0:T(8,128)(2,1)S(1)}, u32[]{:S(2)}, u32[]{:S(2)}) collective-permute-start(bf16[288,256]{1,0:T(8,128)(2,1)S(1)} %pass_on.11), channel_id=1, source_target_pairs={{1,0},{2,1},{3,2},{4,3},{5,4},{6,5},{7,6},{0,7},{9,8},{10,9},{11,1... | collective-permute-start | bytes 442376 | tf_op jit(solution)/shard_map/ppermute | solution.py:392
  110.2 2.0 %collective-permute-done.18.falling.refs_8_ = bf16[288,256]{1,0:T(8,128)(2,1)S(1)} collective-permute-done((bf16[288,256]{1,0:T(8,128)(2,1)S(1)}, bf16[288,256]{1,0:T(8,128)(2,1)S(1)}, u32[]{:S(2)}, u32[]{:S(2)}) %collective-permute-start.18) | collective-permute-done | bytes 147488 | tf_op jit(solution)/shard_map/ppermute | solution.py:392
  112.2 3.2 %collective-permute-done.14.rising.refs_7_ = bf16[288,256]{1,0:T(8,128)(2,1)S(1)} collective-permute-done((bf16[288,256]{1,0:T(8,128)(2,1)S(1)}, bf16[288,256]{1,0:T(8,128)(2,1)S(1)}, u32[]{:S(2)}, u32[]{:S(2)}) %collective-permute-start.14) | collective-permute-done | bytes 147488 | tf_op jit(solution)/shard_map/ppermute | solution.py:391
  116.3 14.1 %all-to-all-start.1 = ((bf16[16,32,256]{2,1,0:T(8,128)(2,1)}), bf16[16,32,256]{2,1,0:T(8,128)(2,1)S(1)}, u32[]{:S(2)}, u32[]{:S(2)}) async-start(bf16[16,32,256]{2,1,0:T(8,128)(2,1)} %ring_sum.1), calls=%async_computation.1 | async-start | bytes 524288 | tf_op jit(solution)/shard_map/all_to_all | solution.py:355
  130.3 5.9 %spmm_back.1 = (bf16[2048,256]{1,0:T(8,128)(2,1)S(1)}, bf16[2048,256]{1,0:T(8,128)(2,1)S(1)}) custom-call(s32[1]{0:T(128)} %bitcast.12.live, s32[160]{0:T(256)S(1)} %get-tuple-element.69.src.dst, s32[160]{0:T(256)S(1)} %get-tuple-element.65.src, bf16[512,256]{1,0:T(8,128)(2,1)S(1)} %get-tuple-element.51.refs_0_, ...), custom_call_target="tpu_custom_call" | custom-call | flops 13421772800 | bytes 37748736 | tf_op jit(solution)/shard_map/spmm_back/pallas_call | solution.py:104
  137.2 1.8 %all-to-all-done.1.parts = bf16[16,32,256]{2,1,0:T(8,128)(2,1)S(1)} async-done(((bf16[16,32,256]{2,1,0:T(8,128)(2,1)}), bf16[16,32,256]{2,1,0:T(8,128)(2,1)S(1)}, u32[]{:S(2)}, u32[]{:S(2)}) %all-to-all-start.1) | async-done | bytes 262176 | tf_op jit(solution)/shard_map/all_to_all | solution.py:355
  140.2 2.5 %collective-permute-done.26.second = bf16[2048,256]{1,0:T(8,128)(2,1)S(1)} collective-permute-done((bf16[2048,256]{1,0:T(8,128)(2,1)}, bf16[2048,256]{1,0:T(8,128)(2,1)S(1)}, u32[]{:S(2)}, u32[]{:S(2)}) %collective-permute-start.26) | collective-permute-done | bytes 1048608 | tf_op jit(solution)/shard_map/ppermute | solution.py:405
  143.9 3.9 %all-to-all-start.2 = ((bf16[8,256,256]{2,1,0:T(8,128)(2,1)}), bf16[8,256,256]{2,1,0:T(8,128)(2,1)S(1)}, u32[]{:S(2)}, u32[]{:S(2)}) async-start(bf16[8,256,256]{2,1,0:T(8,128)(2,1)} %bitcast.9), calls=%async_computation.2 | async-start | bytes 2097152 | tf_op jit(solution)/shard_map/all_to_all | solution.py:355
  148.7 4.7 %collective-permute-start.22 = (f32[32,256]{1,0:T(8,128)S(1)}, f32[32,256]{1,0:T(8,128)S(1)}, u32[]{:S(2)}, u32[]{:S(2)}) collective-permute-start(f32[32,256]{1,0:T(8,128)S(1)} %scaled_sum.1.refs_0_), channel_id=1, source_target_pairs={{0,4},{1,5},{2,6},{3,7},{4,0},{5,1},{6,2},{7,3},{8,12},{9,13},{10,... | collective-permute-start | bytes 98312 | tf_op jit(solution)/shard_map/ppermute | solution.py:410
  153.5 2.0 %collective-permute-start.21 = (f32[32,256]{1,0:T(8,128)S(1)}, f32[32,256]{1,0:T(8,128)S(1)}, u32[]{:S(2)}, u32[]{:S(2)}) collective-permute-start(f32[32,256]{1,0:T(8,128)S(1)} %scaled_sum.1.refs_0_), channel_id=1, source_target_pairs={{0,5},{1,6},{2,7},{3,0},{4,1},{5,2},{6,3},{7,4},{8,13},{9,14},{10,... | collective-permute-start | bytes 98312 | tf_op jit(solution)/shard_map/ppermute | solution.py:410
  158.3 2.7 %collective-permute-done.20.refs_2_ = f32[32,256]{1,0:T(8,128)S(1)} collective-permute-done((f32[32,256]{1,0:T(8,128)S(1)}, f32[32,256]{1,0:T(8,128)S(1)}, u32[]{:S(2)}, u32[]{:S(2)}) %collective-permute-start.20) | collective-permute-done | bytes 32800 | tf_op jit(solution)/shard_map/ppermute | solution.py:410
  162.3 2.1 %all-to-all-done.2.parts = bf16[8,256,256]{2,1,0:T(8,128)(2,1)S(1)} async-done(((bf16[8,256,256]{2,1,0:T(8,128)(2,1)}), bf16[8,256,256]{2,1,0:T(8,128)(2,1)S(1)}, u32[]{:S(2)}, u32[]{:S(2)}) %all-to-all-start.2) | async-done | bytes 1048608 | tf_op jit(solution)/shard_map/all_to_all | solution.py:355
  (60 shorter events, 19.2 us)
Async XLA Ops:
  26.5 4.2 %collective-permute-start = (bf16[2048,256]{1,0:T(8,128)(2,1)S(1)}, bf16[2048,256]{1,0:T(8,128)(2,1)S(1)}, u32[]{:S(2)}, u32[]{:S(2)}) collective-permute-start(bf16[2048,256]{1,0:T(8,128)(2,1)S(1)} %bitcast.13), channel_id=1, source_target_pairs={{0,16},{16,0},{32,48},{48,32},{64,80},{80,64},{96,112},{112,96},{1... | collective-permute-start | bytes 3145736 | tf_op jit(solution)/shard_map/ppermute | solution.py:361
  36.3 38.9 %copy-start.1 = (bf16[256,256]{1,0:T(8,128)(2,1)S(1)}, bf16[256,256]{1,0:T(8,128)(2,1)}, u32[]{:S(2)}) copy-start(bf16[256,256]{1,0:T(8,128)(2,1)} %weight.1) | copy-start | bytes 393220
  36.3 38.8 %copy-start.2 = (bf16[1,256,256]{2,1,0:T(8,128)(2,1)S(1)}, bf16[1,256,256]{2,1,0:T(8,128)(2,1)}, u32[]{:S(2)}) copy-start(bf16[1,256,256]{2,1,0:T(8,128)(2,1)} %param.13) | copy-start | bytes 393220
  36.3 8.1 %collective-permute-start.5 = (bf16[256,256]{1,0:T(8,128)(2,1)S(1)}, bf16[256,256]{1,0:T(8,128)(2,1)S(1)}, u32[]{:S(2)}, u32[]{:S(2)}) collective-permute-start(bf16[256,256]{1,0:T(8,128)(2,1)S(1)} %get-tuple-element.42), channel_id=1, source_target_pairs={{1,0},{2,1},{3,2},{4,3},{5,4},{6,5},{7,6},{0,7},{9,8},{10,9},{11,1... | collective-permute-start | bytes 393224 | tf_op jit(solution)/shard_map/ppermute | solution.py:370
  41.3 6.7 %collective-permute-start.1 = (bf16[256,256]{1,0:T(8,128)(2,1)S(1)}, bf16[256,256]{1,0:T(8,128)(2,1)S(1)}, u32[]{:S(2)}, u32[]{:S(2)}) collective-permute-start(bf16[256,256]{1,0:T(8,128)(2,1)S(1)} %get-tuple-element.38), channel_id=1, source_target_pairs={{0,1},{1,2},{2,3},{3,4},{4,5},{5,6},{6,7},{7,0},{8,9},{9,10},{10,1... | collective-permute-start | bytes 393224 | tf_op jit(solution)/shard_map/ppermute | solution.py:369
  44.5 8.6 %collective-permute-start.6 = (bf16[512,256]{1,0:T(8,128)(2,1)S(1)}, bf16[512,256]{1,0:T(8,128)(2,1)S(1)}, u32[]{:S(2)}, u32[]{:S(2)}) collective-permute-start(bf16[512,256]{1,0:T(8,128)(2,1)S(1)} %add_at.10), channel_id=1, source_target_pairs={{1,0},{2,1},{3,2},{4,3},{5,4},{6,5},{7,6},{0,7},{9,8},{10,9},{11,1... | collective-permute-start | bytes 786440 | tf_op jit(solution)/shard_map/ppermute | solution.py:370
  48.0 8.7 %collective-permute-start.2 = (bf16[512,256]{1,0:T(8,128)(2,1)S(1)}, bf16[512,256]{1,0:T(8,128)(2,1)S(1)}, u32[]{:S(2)}, u32[]{:S(2)}) collective-permute-start(bf16[512,256]{1,0:T(8,128)(2,1)S(1)} %add_at.7), channel_id=1, source_target_pairs={{0,1},{1,2},{2,3},{3,4},{4,5},{5,6},{6,7},{7,0},{8,9},{9,10},{10,1... | collective-permute-start | bytes 786440 | tf_op jit(solution)/shard_map/ppermute | solution.py:369
  53.2 7.7 %collective-permute-start.7 = (bf16[512,256]{1,0:T(8,128)(2,1)S(1)}, bf16[512,256]{1,0:T(8,128)(2,1)S(1)}, u32[]{:S(2)}, u32[]{:S(2)}) collective-permute-start(bf16[512,256]{1,0:T(8,128)(2,1)S(1)} %add_at.11), channel_id=1, source_target_pairs={{1,0},{2,1},{3,2},{4,3},{5,4},{6,5},{7,6},{0,7},{9,8},{10,9},{11,1... | collective-permute-start | bytes 786440 | tf_op jit(solution)/shard_map/ppermute | solution.py:370
  56.7 7.7 %collective-permute-start.3 = (bf16[512,256]{1,0:T(8,128)(2,1)S(1)}, bf16[512,256]{1,0:T(8,128)(2,1)S(1)}, u32[]{:S(2)}, u32[]{:S(2)}) collective-permute-start(bf16[512,256]{1,0:T(8,128)(2,1)S(1)} %add_at.8), channel_id=1, source_target_pairs={{0,1},{1,2},{2,3},{3,4},{4,5},{5,6},{6,7},{7,0},{8,9},{9,10},{10,1... | collective-permute-start | bytes 786440 | tf_op jit(solution)/shard_map/ppermute | solution.py:369
  61.0 6.8 %collective-permute-start.8 = (bf16[512,256]{1,0:T(8,128)(2,1)S(1)}, bf16[512,256]{1,0:T(8,128)(2,1)S(1)}, u32[]{:S(2)}, u32[]{:S(2)}) collective-permute-start(bf16[512,256]{1,0:T(8,128)(2,1)S(1)} %add_at.12), channel_id=1, source_target_pairs={{1,0},{2,1},{3,2},{4,3},{5,4},{6,5},{7,6},{0,7},{9,8},{10,9},{11,1... | collective-permute-start | bytes 786440 | tf_op jit(solution)/shard_map/ppermute | solution.py:374
  64.5 6.5 %collective-permute-start.4 = (bf16[512,256]{1,0:T(8,128)(2,1)S(1)}, bf16[512,256]{1,0:T(8,128)(2,1)S(1)}, u32[]{:S(2)}, u32[]{:S(2)}) collective-permute-start(bf16[512,256]{1,0:T(8,128)(2,1)S(1)} %add_at.9), channel_id=1, source_target_pairs={{0,1},{1,2},{2,3},{3,4},{4,5},{5,6},{6,7},{7,0},{8,9},{9,10},{10,1... | collective-permute-start | bytes 786440 | tf_op jit(solution)/shard_map/ppermute | solution.py:373
  71.1 4.0 %collective-permute-start.9 = (bf16[256,256]{1,0:T(8,128)(2,1)S(1)}, bf16[256,256]{1,0:T(8,128)(2,1)S(1)}, u32[]{:S(2)}, u32[]{:S(2)}) collective-permute-start(bf16[256,256]{1,0:T(8,128)(2,1)S(1)} %get-tuple-element.44), channel_id=1, source_target_pairs={{0,8},{1,9},{2,10},{3,11},{4,12},{5,13},{6,14},{7,15},{8,0},{9,1},... | collective-permute-start | bytes 393224 | tf_op jit(solution)/shard_map/ppermute | solution.py:376
  76.1 6.0 %collective-permute-start.10 = (bf16[512,256]{1,0:T(8,128)(2,1)S(1)}, bf16[512,256]{1,0:T(8,128)(2,1)S(1)}, u32[]{:S(2)}, u32[]{:S(2)}) collective-permute-start(bf16[512,256]{1,0:T(8,128)(2,1)S(1)} %get-tuple-element.46.sent), channel_id=1, source_target_pairs={{0,8},{1,9},{2,10},{3,11},{4,12},{5,13},{6,14},{7,15},{8,0},{9,1},... | collective-permute-start | bytes 786440 | tf_op jit(solution)/shard_map/ppermute | solution.py:380
  82.1 9.5 %collective-permute-start.11 = (bf16[544,256]{1,0:T(8,128)(2,1)S(1)}, bf16[544,256]{1,0:T(8,128)(2,1)S(1)}, u32[]{:S(2)}, u32[]{:S(2)}) collective-permute-start(bf16[544,256]{1,0:T(8,128)(2,1)S(1)} %get-tuple-element.47), channel_id=1, source_target_pairs={{0,1},{1,2},{2,3},{3,4},{4,5},{5,6},{6,7},{7,0},{8,9},{9,10},{10,1... | collective-permute-start | bytes 835592 | tf_op jit(solution)/shard_map/ppermute | solution.py:385
  82.2 6.0 %collective-permute-start.15 = (bf16[512,256]{1,0:T(8,128)(2,1)S(1)}, bf16[512,256]{1,0:T(8,128)(2,1)S(1)}, u32[]{:S(2)}, u32[]{:S(2)}) collective-permute-start(bf16[512,256]{1,0:T(8,128)(2,1)S(1)} %get-tuple-element.51.refs_0_), channel_id=1, source_target_pairs={{1,0},{2,1},{3,2},{4,3},{5,4},{6,5},{7,6},{0,7},{9,8},{10,9},{11,1... | collective-permute-start | bytes 786440 | tf_op jit(solution)/shard_map/ppermute | solution.py:386
  88.2 9.7 %collective-permute-start.16 = (bf16[544,256]{1,0:T(8,128)(2,1)S(1)}, bf16[544,256]{1,0:T(8,128)(2,1)S(1)}, u32[]{:S(2)}, u32[]{:S(2)}) collective-permute-start(bf16[544,256]{1,0:T(8,128)(2,1)S(1)} %pass_on.9), channel_id=1, source_target_pairs={{1,0},{2,1},{3,2},{4,3},{5,4},{6,5},{7,6},{0,7},{9,8},{10,9},{11,1... | collective-permute-start | bytes 835592 | tf_op jit(solution)/shard_map/ppermute | solution.py:386
  91.6 9.6 %collective-permute-start.12 = (bf16[544,256]{1,0:T(8,128)(2,1)S(1)}, bf16[544,256]{1,0:T(8,128)(2,1)S(1)}, u32[]{:S(2)}, u32[]{:S(2)}) collective-permute-start(bf16[544,256]{1,0:T(8,128)(2,1)S(1)} %pass_on.6), channel_id=1, source_target_pairs={{0,1},{1,2},{2,3},{3,4},{4,5},{5,6},{6,7},{7,0},{8,9},{9,10},{10,1... | collective-permute-start | bytes 835592 | tf_op jit(solution)/shard_map/ppermute | solution.py:385
  97.9 8.7 %collective-permute-start.17 = (bf16[544,256]{1,0:T(8,128)(2,1)S(1)}, bf16[544,256]{1,0:T(8,128)(2,1)S(1)}, u32[]{:S(2)}, u32[]{:S(2)}) collective-permute-start(bf16[544,256]{1,0:T(8,128)(2,1)S(1)} %pass_on.10), channel_id=1, source_target_pairs={{1,0},{2,1},{3,2},{4,3},{5,4},{6,5},{7,6},{0,7},{9,8},{10,9},{11,1... | collective-permute-start | bytes 835592 | tf_op jit(solution)/shard_map/ppermute | solution.py:386
  101.2 8.9 %collective-permute-start.13 = (bf16[544,256]{1,0:T(8,128)(2,1)S(1)}, bf16[544,256]{1,0:T(8,128)(2,1)S(1)}, u32[]{:S(2)}, u32[]{:S(2)}) collective-permute-start(bf16[544,256]{1,0:T(8,128)(2,1)S(1)} %pass_on.7), channel_id=1, source_target_pairs={{0,1},{1,2},{2,3},{3,4},{4,5},{5,6},{6,7},{7,0},{8,9},{9,10},{10,1... | collective-permute-start | bytes 835592 | tf_op jit(solution)/shard_map/ppermute | solution.py:385
  106.6 5.6 %collective-permute-start.18 = (bf16[288,256]{1,0:T(8,128)(2,1)S(1)}, bf16[288,256]{1,0:T(8,128)(2,1)S(1)}, u32[]{:S(2)}, u32[]{:S(2)}) collective-permute-start(bf16[288,256]{1,0:T(8,128)(2,1)S(1)} %pass_on.11), channel_id=1, source_target_pairs={{1,0},{2,1},{3,2},{4,3},{5,4},{6,5},{7,6},{0,7},{9,8},{10,9},{11,1... | collective-permute-start | bytes 442376 | tf_op jit(solution)/shard_map/ppermute | solution.py:392
  110.1 5.3 %collective-permute-start.14 = (bf16[288,256]{1,0:T(8,128)(2,1)S(1)}, bf16[288,256]{1,0:T(8,128)(2,1)S(1)}, u32[]{:S(2)}, u32[]{:S(2)}) collective-permute-start(bf16[288,256]{1,0:T(8,128)(2,1)S(1)} %pass_on.8), channel_id=1, source_target_pairs={{0,1},{1,2},{2,3},{3,4},{4,5},{5,6},{6,7},{7,0},{8,9},{9,10},{10,1... | collective-permute-start | bytes 442376 | tf_op jit(solution)/shard_map/ppermute | solution.py:391
  116.3 22.8 %all-to-all-start.1 = ((bf16[16,32,256]{2,1,0:T(8,128)(2,1)}), bf16[16,32,256]{2,1,0:T(8,128)(2,1)S(1)}, u32[]{:S(2)}, u32[]{:S(2)}) async-start(bf16[16,32,256]{2,1,0:T(8,128)(2,1)} %ring_sum.1), calls=%async_computation.1 | async-start | bytes 524288 | tf_op jit(solution)/shard_map/all_to_all | solution.py:355
  136.2 1.0 copy-start.3
  139.1 3.6 %collective-permute-start.26 = (bf16[2048,256]{1,0:T(8,128)(2,1)}, bf16[2048,256]{1,0:T(8,128)(2,1)S(1)}, u32[]{:S(2)}, u32[]{:S(2)}) collective-permute-start(bf16[2048,256]{1,0:T(8,128)(2,1)} %copy-done.3), channel_id=1, source_target_pairs={{0,16},{16,0},{32,48},{48,32},{64,80},{80,64},{96,112},{112,96},{1... | collective-permute-start | bytes 3145736 | tf_op jit(solution)/shard_map/ppermute | solution.py:405
  143.9 20.5 %all-to-all-start.2 = ((bf16[8,256,256]{2,1,0:T(8,128)(2,1)}), bf16[8,256,256]{2,1,0:T(8,128)(2,1)S(1)}, u32[]{:S(2)}, u32[]{:S(2)}) async-start(bf16[8,256,256]{2,1,0:T(8,128)(2,1)} %bitcast.9), calls=%async_computation.2 | async-start | bytes 2097152 | tf_op jit(solution)/shard_map/all_to_all | solution.py:355
  147.8 7.6 %collective-permute-start.25 = (f32[32,256]{1,0:T(8,128)S(1)}, f32[32,256]{1,0:T(8,128)S(1)}, u32[]{:S(2)}, u32[]{:S(2)}) collective-permute-start(f32[32,256]{1,0:T(8,128)S(1)} %scaled_sum.1.refs_0_), channel_id=1, source_target_pairs={{0,1},{1,2},{2,3},{3,4},{4,5},{5,6},{6,7},{7,0},{8,9},{9,10},{10,1... | collective-permute-start | bytes 98312 | tf_op jit(solution)/shard_map/ppermute | solution.py:410
  147.8 9.2 %collective-permute-start.24 = (f32[32,256]{1,0:T(8,128)S(1)}, f32[32,256]{1,0:T(8,128)S(1)}, u32[]{:S(2)}, u32[]{:S(2)}) collective-permute-start(f32[32,256]{1,0:T(8,128)S(1)} %scaled_sum.1.refs_0_), channel_id=1, source_target_pairs={{0,2},{1,3},{2,4},{3,5},{4,6},{5,7},{6,0},{7,1},{8,10},{9,11},{10,... | collective-permute-start | bytes 98312 | tf_op jit(solution)/shard_map/ppermute | solution.py:410
  147.9 10.1 %collective-permute-start.23 = (f32[32,256]{1,0:T(8,128)S(1)}, f32[32,256]{1,0:T(8,128)S(1)}, u32[]{:S(2)}, u32[]{:S(2)}) collective-permute-start(f32[32,256]{1,0:T(8,128)S(1)} %scaled_sum.1.refs_0_), channel_id=1, source_target_pairs={{0,3},{1,4},{2,5},{3,6},{4,7},{5,0},{6,1},{7,2},{8,11},{9,12},{10,... | collective-permute-start | bytes 98312 | tf_op jit(solution)/shard_map/ppermute | solution.py:410
  148.7 9.2 %collective-permute-start.22 = (f32[32,256]{1,0:T(8,128)S(1)}, f32[32,256]{1,0:T(8,128)S(1)}, u32[]{:S(2)}, u32[]{:S(2)}) collective-permute-start(f32[32,256]{1,0:T(8,128)S(1)} %scaled_sum.1.refs_0_), channel_id=1, source_target_pairs={{0,4},{1,5},{2,6},{3,7},{4,0},{5,1},{6,2},{7,3},{8,12},{9,13},{10,... | collective-permute-start | bytes 98312 | tf_op jit(solution)/shard_map/ppermute | solution.py:410
  153.5 4.9 %collective-permute-start.21 = (f32[32,256]{1,0:T(8,128)S(1)}, f32[32,256]{1,0:T(8,128)S(1)}, u32[]{:S(2)}, u32[]{:S(2)}) collective-permute-start(f32[32,256]{1,0:T(8,128)S(1)} %scaled_sum.1.refs_0_), channel_id=1, source_target_pairs={{0,5},{1,6},{2,7},{3,0},{4,1},{5,2},{6,3},{7,4},{8,13},{9,14},{10,... | collective-permute-start | bytes 98312 | tf_op jit(solution)/shard_map/ppermute | solution.py:410
  155.4 5.5 %collective-permute-start.20 = (f32[32,256]{1,0:T(8,128)S(1)}, f32[32,256]{1,0:T(8,128)S(1)}, u32[]{:S(2)}, u32[]{:S(2)}) collective-permute-start(f32[32,256]{1,0:T(8,128)S(1)} %scaled_sum.1.refs_0_), channel_id=1, source_target_pairs={{0,6},{1,7},{2,0},{3,1},{4,2},{5,3},{6,4},{7,5},{8,14},{9,15},{10,... | collective-permute-start | bytes 98312 | tf_op jit(solution)/shard_map/ppermute | solution.py:410
  157.0 4.6 %collective-permute-start.19 = (f32[32,256]{1,0:T(8,128)S(1)}, f32[32,256]{1,0:T(8,128)S(1)}, u32[]{:S(2)}, u32[]{:S(2)}) collective-permute-start(f32[32,256]{1,0:T(8,128)S(1)} %scaled_sum.1.refs_0_), channel_id=1, source_target_pairs={{0,7},{1,0},{2,1},{3,2},{4,3},{5,4},{6,5},{7,6},{8,15},{9,8},{10,9... | collective-permute-start | bytes 98312 | tf_op jit(solution)/shard_map/ppermute | solution.py:410
  (1 other events, 0.9 us)

commit v3 on v2

--- a/solution.py
+++ b/solution.py
@@ -32,22 +32,6 @@
         copy.start()
     for copy in copies:
         copy.wait()
-
-
-def spread_kernel(source, out, sems):
-    copy_all([(source, out.at[i]) for i in range(out.shape[0])], sems)
-
-
-def spread(source, copies):
-    return pl.pallas_call(
-        spread_kernel,
-        out_shape=shape(source.dtype, copies, *source.shape),
-        in_specs=[VMEM],
-        out_specs=HBM,
-        scratch_shapes=[DMA((copies,))],
-        compiler_params=params(4),
-        name="spread",
-    )(source)
 
 
 def spmm_kernel(transposed, pieces, live, dst, src, *refs):
@@ -120,24 +104,43 @@
     )(live, dst, src, *sources, pltpu.with_memory_space_constraint(tiles, pltpu.HBM))
 
 
-def add_at_kernel(start, first, second, out):
-    end = start + second.shape[0]
-    out[start:end, :] = (first[start:end, :].astype(jnp.float32) + f32(second)).astype(out.dtype)
-    if start > 0:
-        out[:start, :] = first[:start, :]
-    if end < out.shape[0]:
-        out[end:, :] = first[end:, :]
-
-
-def add_at(first, second, start=0):
-    return pl.pallas_call(
-        functools.partial(add_at_kernel, start),
+def add_kernel(first, second, out):
+    out[...] = (f32(first) + f32(second)).astype(out.dtype)
+
+
+def add(first, second):
+    return pl.pallas_call(
+        add_kernel,
         out_shape=shape(first.dtype, *first.shape),
         in_specs=[VMEM] * 2,
         out_specs=VMEM,
         compiler_params=params(6),
-        name="add_at",
+        name="add",
     )(first, second)
+
+
+def ring_add_kernel(upper, rising, lower, falling, rising_out, falling_out):
+    end = rising.shape[0]
+    rising_out[:end, :] = (upper[:end, :].astype(jnp.float32) + f32(rising)).astype(upper.dtype)
+    if end < upper.shape[0]:
+        rising_out[end:, :] = upper[end:, :]
+    start = lower.shape[0] - falling.shape[0]
+    falling_out[start:, :] = (lower[start:, :].astype(jnp.float32) + f32(falling)).astype(
+        lower.dtype
+    )
+    if start > 0:
+        falling_out[:start, :] = lower[:start, :]
+
+
+def ring_add(upper, rising, lower, falling):
+    return pl.pallas_call(
+        ring_add_kernel,
+        out_shape=[shape(upper.dtype, *upper.shape)] * 2,
+        in_specs=[VMEM] * 4,
+        out_specs=[VMEM] * 2,
+        compiler_params=params(8),
+        name="ring_add",
+    )(upper, rising, lower, falling)
 
 
 def part_sum(parts):
@@ -147,21 +150,18 @@
     return sums
 
 
-def split_sum_kernel(own, first, second, mine, theirs):
-    sums = f32(own) + f32(first) + f32(second)
-    mine[...] = sums[: mine.shape[0]]
-    theirs[...] = sums[mine.shape[0] :].astype(theirs.dtype)
-
-
-def split_sum(own, first, second):
-    rows, width = own.shape
-    return pl.pallas_call(
-        split_sum_kernel,
-        out_shape=[shape(jnp.float32, rows // 2, width), shape(own.dtype, rows // 2, width)],
+def fold_kernel(own, first, second, out):
+    out[...] = (f32(own) + f32(first) + f32(second)).astype(out.dtype)
+
+
+def fold(own, first, second):
+    return pl.pallas_call(
+        fold_kernel,
+        out_shape=shape(own.dtype, *own.shape),
         in_specs=[VMEM] * 3,
-        out_specs=[VMEM] * 2,
+        out_specs=VMEM,
         compiler_params=params(4),
-        name="split_sum",
+        name="fold",
     )(own, first, second)
 
 
@@ -180,87 +180,100 @@
     )(parts)
 
 
-def dense_kernel(mine, swapped, weight, cotangent, activated, sent):
-    rows = cotangent.shape[0]
-    aggregated = (mine[...] + f32(swapped)).astype(jnp.bfloat16)
-    pre = jnp.dot(aggregated, weight[...], preferred_element_type=jnp.float32)
-    gate = jax.nn.sigmoid(pre)
-    slope = gate * (1.0 + pre * (1.0 - gate))
-    upstream = (cotangent[...].astype(jnp.float32) * slope).astype(jnp.bfloat16)
-    sent[:rows, :] = lax.dot_general(
-        upstream, weight[...], (((1,), (1,)), ((), ())), preferred_element_type=jnp.float32
-    ).astype(jnp.bfloat16)
-    sent[rows:, :] = lax.dot_general(
-        aggregated, upstream, (((0,), (0,)), ((), ())), preferred_element_type=jnp.float32
-    ).astype(jnp.bfloat16)
-    activated[...] = (pre * gate).astype(jnp.bfloat16)
-
-
-def dense(mine, swapped, weight, cotangent):
-    rows, width = cotangent.shape
-    return pl.pallas_call(
-        dense_kernel,
-        out_shape=[
+def dense_kernel(chain, last, place, own, other, weight, cotangent, other_cotangent, *refs):
+    rows = own.shape[0] // 2
+    at_rows = slice(chain * rows, (chain + 1) * rows)
+    if last:
+        before, pair_before, terms_before, activated, pair, rising, sums = refs
+        activated[: chain * rows, :] = before[...]
+    else:
+        activated, pair, terms_out = refs
+    terms = []
+    for at, cot in ((0, cotangent), (rows, other_cotangent)):
+        there = rows - at
+        aggregated = (
+            own[at : at + rows, :].astype(jnp.float32)
+            + other[there : there + rows, :].astype(jnp.float32)
+        ).astype(jnp.bfloat16)
+        pre = jnp.dot(aggregated, weight[...], preferred_element_type=jnp.float32)
+        gate = jax.nn.sigmoid(pre)
+        slope = gate * (1.0 + pre * (1.0 - gate))
+        upstream = (cot[at_rows, :].astype(jnp.float32) * slope).astype(jnp.bfloat16)
+        down = lax.dot_general(
+            upstream, weight[...], (((1,), (1,)), ((), ())), preferred_element_type=jnp.float32
+        ).astype(jnp.bfloat16)
+        if last:
+            for out in (pair, rising):
+                out[2 * at : 2 * at + rows, :] = pair_before[at : at + rows, :]
+                out[2 * at + rows : 2 * at + 2 * rows, :] = down
+        else:
+            pair[at : at + rows, :] = down
+        terms.append(
+            lax.dot_general(
+                aggregated, upstream, (((0,), (0,)), ((), ())), preferred_element_type=jnp.float32
+            )
+        )
+        if at == 0:
+            activated[at_rows if last else slice(None), :] = (pre * gate).astype(jnp.bfloat16)
+    total = terms[0] + terms[1]
+    if last:
+        along = sums.shape[0]
+        sums[...] = (terms_before[...] + total).reshape(sums.shape)
+        far = lax.rem(place[0] + along // 2, along)
+        rising[pair.shape[0] :, :] = sums[far].astype(rising.dtype)
+    else:
+        terms_out[...] = total
+
+
+def dense(chain, place, own, other, weight, cotangent, other_cotangent, along, before=()):
+    rows, width = own.shape[0] // 2, own.shape[1]
+    part = width // along
+    if before:
+        out = [
+            shape(jnp.bfloat16, 2 * rows, width),
+            shape(jnp.bfloat16, 4 * rows, width),
+            shape(jnp.bfloat16, 4 * rows + part, width),
+            shape(jnp.float32, along, part, width),
+        ]
+    else:
+        out = [
             shape(jnp.bfloat16, rows, width),
-            shape(jnp.bfloat16, rows + width, width),
-        ],
-        in_specs=[VMEM] * 4,
+            shape(jnp.bfloat16, 2 * rows, width),
+            shape(jnp.float32, width, width),
+        ]
+    return pl.pallas_call(
+        functools.partial(dense_kernel, chain, bool(before)),
+        out_shape=out,
+        in_specs=[SMEM] + [VMEM] * (5 + len(before)),
+        out_specs=[VMEM] * len(out),
+        compiler_params=params(16),
+        name="dense",
+    )(place, own, other, weight, cotangent, other_cotangent, *before)
+
+
+def pass_on_kernel(cut, offsets, held, place, rising, falling, sums, rising_out, falling_out):
+    along, part = sums.shape[:2]
+    for first, last, offset, arrived, out in (
+        (0, held - cut, offsets[0], rising, rising_out),
+        (cut, held, offsets[1], falling, falling_out),
+    ):
+        out[: last - first, :] = arrived[first:last, :]
+        term = sums[lax.rem(place[0] + offset, along)]
+        if arrived.shape[0] > held:
+            term += arrived[held:, :].astype(jnp.float32)
+        out[last - first :, :] = term.astype(out.dtype)
+
+
+def pass_on(cut, offsets, held, place, rising, falling, sums):
+    _, part, width = sums.shape
+    return pl.pallas_call(
+        functools.partial(pass_on_kernel, cut, offsets, held),
+        out_shape=[shape(rising.dtype, held - cut + part, width)] * 2,
+        in_specs=[SMEM] + [VMEM] * 3,
         out_specs=[VMEM] * 2,
-        compiler_params=params(12),
-        name="dense",
-    )(mine, swapped, weight, cotangent)
-
-
-def begin_kernel(place, sent, received, pair, rising, sums):
-    rows = pair.shape[0] // 2
-    along, part = sums.shape[:2]
-    for out in (pair, rising):
-        out[:rows, :] = sent[:rows, :]
-        out[rows : 2 * rows, :] = received[:rows, :]
-    for i in range(along):
-        at = slice(rows + i * part, rows + (i + 1) * part)
-        sums[i] = sent[at, :].astype(jnp.float32) + received[at, :].astype(jnp.float32)
-    far = lax.rem(place[0] + along // 2, along)
-    rising[2 * rows :, :] = sums[far].astype(rising.dtype)
-
-
-def begin(place, sent, received, rows, along):
-    width = sent.shape[1]
-    part = (sent.shape[0] - rows) // along
-    return pl.pallas_call(
-        begin_kernel,
-        out_shape=[
-            shape(sent.dtype, 2 * rows, width),
-            shape(sent.dtype, 2 * rows + part, width),
-            shape(jnp.float32, along, part, width),
-        ],
-        in_specs=[SMEM] + [VMEM] * 2,
-        out_specs=[VMEM] * 3,
         compiler_params=params(8),
-        name="begin",
-    )(place, sent, received)
-
-
-def pass_on_kernel(first, last, offset, held, place, arrived, sums, out):
-    rows = last - first
-    along, part = sums.shape[:2]
-    out[:rows, :] = arrived[first:last, :]
-    term = sums[lax.rem(place[0] + offset, along)]
-    if arrived.shape[0] > held:
-        term += arrived[held:, :].astype(jnp.float32)
-    out[rows:, :] = term.astype(out.dtype)
-
-
-def pass_on(first, last, offset, held, place, arrived, sums):
-    _, part, width = sums.shape
-    return pl.pallas_call(
-        functools.partial(pass_on_kernel, first, last, offset, held),
-        out_shape=shape(arrived.dtype, last - first + part, width),
-        in_specs=[SMEM] + [VMEM] * 2,
-        out_specs=VMEM,
-        compiler_params=params(6),
         name="pass_on",
-    )(place, arrived, sums)
+    )(place, rising, falling, sums)
 
 
 def ring_sum_kernel(place, rising, falling, sums, out, stage, sems):
@@ -348,8 +361,9 @@
         distance == 0, along - 1,
         jnp.where(distance <= far, along - 1 - 2 * distance + (distance == far), 2 * distance - along),
     )
-    within = ((row_owner // along) ^ side) * per + row_inner
-    by_nearest, by_farthest = nearest * 2 * per + within, farthest * 2 * per + within
+    row_side = (row_owner // along) ^ side
+    by_nearest = (nearest * 2 + row_side) * per + row_inner
+    by_farthest = (row_inner * along + farthest) * 2 + row_side
 
     def exchange(x, axis, groups=None):
         return lax.all_to_all(x, axis, 0, 0, axis_index_groups=groups, tiled=True)
@@ -357,28 +371,42 @@
     def flat(x):
         return x.reshape(-1, x.shape[-1])
 
-    own = flat(exchange(spread(features.reshape(node_rows, width), chips), "row", same_core))
+    own = flat(
+        exchange(jnp.broadcast_to(features, (chips, node_rows, width)), "row", same_core)
+    )
     other = lax.ppermute(own, "row", core_swap)
+    pair = 2 * tile
+    sizes = [tile] * 2 + [pair] * (along - 1)
+    blocks = spmm(
+        False, live, by_farthest, by_core, [own, other], [chips * node_rows] * 2, tiles, sizes * per
+    )
+    chains = range(per)
+    blocks = [blocks[c * len(sizes) : (c + 1) * len(sizes)] for c in chains]
+    cotangent = cotangent.reshape(node_rows, width)
+    other_cotangent = lax.ppermute(cotangent, "col", side_swap)
+    rings = [(blocks[c][0], blocks[c][1]) for c in chains]
+
+    def turn(ring):
+        return lax.ppermute(ring[0], "col", up), lax.ppermute(ring[1], "col", back)
+
+    for step in range(1, far):
+        for c in chains:
+            rising, falling = turn(rings[c])
+            if step == 1 and c == 0:
+                rising, falling, other_cotangent = lax.optimization_barrier(
+                    (rising, falling, other_cotangent)
+                )
+            rings[c] = ring_add(blocks[c][2 * step], rising, blocks[c][2 * step + 1], falling)
+    own_sums = [fold(blocks[c][-1], *turn(rings[c])) for c in chains]
+    other_sums = [lax.ppermute(own_sums[c], "col", side_swap) for c in chains]
+    spot = place.reshape(1)
+    dense_args = (weight, cotangent, other_cotangent, along)
+    first = dense(0, spot, own_sums[0], other_sums[0], *dense_args)
+    activated, both, rising, sums = dense(
+        1, spot, own_sums[1], other_sums[1], *dense_args, first
+    )
+
     pair = 2 * node_rows
-    blocks = spmm(
-        False, live, by_farthest, by_core, [own, other], [chips * node_rows] * 2, tiles,
-        [node_rows] * 2 + [pair] * (along - 1),
-    )
-    rising, falling = blocks[0], blocks[1]
-    for step in range(1, far):
-        rising = lax.ppermute(rising, "col", up)
-        falling = lax.ppermute(falling, "col", back)
-        rising = add_at(blocks[2 * step], rising)
-        falling = add_at(blocks[2 * step + 1], falling, pair - falling.shape[0])
-    rising = lax.ppermute(rising, "col", up)
-    falling = lax.ppermute(falling, "col", back)
-    mine, theirs = split_sum(blocks[-1], rising, falling)
-    swapped = lax.ppermute(theirs, "col", side_swap)
-    spot = place.reshape(1)
-    activated, sent = dense(mine, swapped, weight, cotangent.reshape(node_rows, width))
-
-    received = lax.ppermute(sent, "col", side_swap)
-    both, rising, sums = begin(spot, sent, received, node_rows, along)
     falling = both
     sources = [both]
     for step in range(1, far):
@@ -386,33 +414,34 @@
         falling = lax.ppermute(falling, "col", back)
         sources += [rising, falling]
         cut = node_rows if step == far - 1 else 0
-        rising = pass_on(0, pair - cut, far - step, pair, spot, rising, sums)
-        falling = pass_on(cut, pair, far + step, pair, spot, falling, sums)
+        rising, falling = pass_on(
+            cut, (far - step, far + step), pair, spot, rising, falling, sums
+        )
     rising = lax.ppermute(rising, "col", up)
     falling = lax.ppermute(falling, "col", back)
     sources += [rising, falling]
-    terms = ring_sum(spot, rising, falling, sums, rows_n)
+    terms = ring_sum(spot, rising, falling, sums, chips)
     terms, *sources = lax.optimization_barrier((terms, *sources))
-    terms = exchange(terms, "row")
+    terms = exchange(terms, "row", same_core)
 
     mine, theirs = spmm(
         True, live, by_core, by_nearest, sources, [pair] * (along - 1) + [node_rows] * 2,
         tiles, [chips * node_rows] * 2,
     )
-    scale = float(node_rows * rows_n * cols_n) ** (-0.5)
-    own_share = scaled_sum(terms, scale)
-    own_share, mine, theirs = lax.optimization_barrier((own_share, mine, theirs))
-    shares = add_at(mine, lax.ppermute(theirs, "row", core_swap))
+    share = scaled_sum(terms, float(node_rows * rows_n * cols_n) ** (-0.5))
+    share, mine, theirs = lax.optimization_barrier((share, mine, theirs))
+    shares = add(mine, lax.ppermute(theirs, "row", core_swap))
+    share = add(share, lax.ppermute(share, "row", core_swap))
     shares = exchange(shares.reshape(chips, node_rows, width), "row", same_core)
     feature_grad = whole_sum(shares)
 
     turned = [
         lax.ppermute(
-            own_share, "col", [(i, i - i % along + (i - turn) % along) for i in range(cols_n)]
+            share, "col", [(i, i - i % along + (i - turn) % along) for i in range(cols_n)]
         )
         for turn in range(1, along)
     ]
-    weight_grad = arrange(spot, [own_share] + turned)
+    weight_grad = arrange(spot, [share] + turned)
     return (
         activated.reshape(1, node_rows, width),
         weight_grad,

time: 165 us -> 154 us (0.933); the launches traced: 165 us -> 152 us
  waiting for transfers between devices: 55.9 us -> 31.3 us
  starting transfers between devices: 63 us -> 76.9 us
  Pallas kernels: 18 us -> 15.7 us
    ppermute x10 -> x28, starting transfers between devices: 14.3 us -> 55.8 us  [the longest x8 23.4 us: turn(): lax.ppermute(ring[1], 'col', back)]
    ppermute x8 -> x4, waiting for transfers between devices: 32.2 us -> 3.44 us  [body(): falling = lax.ppermute(falling, 'col', back)]
    ppermute x8 -> x4, starting transfers between devices: 28.2 us -> 7.75 us  [body(): falling = lax.ppermute(falling, 'col', back)]
    all_to_all x2, starting transfers between devices: 18 us -> 8.28 us  [exchange(): return lax.all_to_all(x, axis, 0, 0, axis_index_groups=groups, tiled=True)]
    ppermute x8 -> x4, waiting for transfers between devices: 6.48 us -> 16 us  [body(): rising = lax.ppermute(rising, 'col', up)]
    all_to_all x2, waiting for transfers between devices: 3.93 us -> 0.8 us  [exchange(): return lax.all_to_all(x, axis, 0, 0, axis_index_groups=groups, tiled=True)]
    ppermute x8 -> x4, starting transfers between devices: 0.59 us -> 3.27 us  [body(): rising = lax.ppermute(rising, 'col', up)]
    ppermute x10 -> x28, waiting for transfers between devices: 13 us -> 11 us  [the longest x7 2.95 us: body(): lax.ppermute(share, 'col', [(i, i - i % along + (i - turn) % along) for i...]
  transfers between devices with their start and end apart: 29 -> 39, of which waited for: 19 -> 15; matrix products, arithmetic and copies ran while one was open for 1% -> 1% of each run, Pallas kernels for 4% -> 8%
where the time goes in v3:
time: 154 us; the launch traced here: 152 us
  starting transfers between devices  76.9 us (50%)
  waiting for transfers between devices  31.3 us (20%)
  blocking collectives  23.6 us (15%)
  Pallas kernels  15.7 us (10%)
  local copies, waits for them, and re-layouts  2.01 us (1%)
    all_to_all x1, blocking collectives, exchange(): return lax.all_to_all(x, axis, 0, 0, axis_index_groups=groups, tiled=True)  23.6 us
    ppermute x8, starting transfers between devices, turn(): lax.ppermute(ring[1], 'col', back)  23.4 us
    ppermute x4, waiting for transfers between devices, body(): rising = lax.ppermute(rising, 'col', up)  16 us
    ppermute x7, starting transfers between devices, body(): lax.ppermute(share, 'col', [(i, i - i % along + (i - turn) % along) for i...  13.2 us
    ppermute x1, starting transfers between devices, body(): shares = add(mine, lax.ppermute(theirs, 'row', core_swap))  11.1 us
    pallas_call x2, Pallas kernels, spmm(): pl.pallas_call(functools.partial(spmm_kernel, transposed, pieces), out_sh...  10.1 us
    all_to_all x2, starting transfers between devices, exchange(): return lax.all_to_all(x, axis, 0, 0, axis_index_groups=groups, tiled=True)  8.28 us
    ppermute x4, starting transfers between devices, body(): falling = lax.ppermute(falling, 'col', back)  7.75 us
  transfers between devices with their start and end apart: 39, of which 15 were waited for; matrix products, arithmetic and copies ran while one was open for 1% of the time, Pallas kernels for 8%

profile of v3, /device:TPU:1, one launch (start us, length us, event | category | flops | bytes accessed | tf_op | source)
XLA Modules:
  0.0 152.3 jit_solution(12080528197761033524)
XLA Ops:
  1.6 23.6 %all_to_all.15 = bf16[8,256,256]{2,1,0:T(8,128)(2,1)S(1)} all-to-all(bf16[8,256,256]{2,1,0:T(8,128)(2,1)S(1)} %broadcast_in_dim.11), channel_id=1, replica_groups={{0,32,64,96,128,160,192,224},{16,48,80,112,144,176,208,240},{1,33,65,97..., dimensions={0} | all-to-all | bytes 2097152 | tf_op jit(solution)/shard_map/all_to_all | solution.py:369
  25.2 1.9 %collective-permute-start = (bf16[2048,256]{1,0:T(8,128)(2,1)S(1)}, bf16[2048,256]{1,0:T(8,128)(2,1)S(1)}, u32[]{:S(2)}, u32[]{:S(2)}) collective-permute-start(bf16[2048,256]{1,0:T(8,128)(2,1)S(1)} %bitcast.13), channel_id=1, source_target_pairs={{0,16},{16,0},{32,48},{48,32},{64,80},{80,64},{96,112},{112,96},{1... | collective-permute-start | bytes 3145736 | tf_op jit(solution)/shard_map/ppermute | solution.py:377
  29.6 4.9 %spmm.1 = (bf16[128,256]{1,0:T(8,128)(2,1)S(1)}, bf16[128,256]{1,0:T(8,128)(2,1)S(1)}, bf16[256,256]{1,0:T(8,128)(2,1)S(1)}, bf16[256,256]{1,0:T(8,128)(2,1)S(1)...) custom-call(s32[1]{0:T(128)} %bitcast.11.live, ...), custom_call_target="tpu_custom_call" | custom-call | flops 13421772800 | bytes 37748736 | tf_op jit(solution)/shard_map/spmm/pallas_call | solution.py:88
  35.5 5.5 %collective-permute-start.11 = (bf16[128,256]{1,0:T(8,128)(2,1)S(1)}, bf16[128,256]{1,0:T(8,128)(2,1)S(1)}, u32[]{:S(2)}, u32[]{:S(2)}) collective-permute-start(bf16[128,256]{1,0:T(8,128)(2,1)S(1)} %get-tuple-element.80), channel_id=1, source_target_pairs={{1,0},{2,1},{3,2},{4,3},{5,4},{6,5},{7,6},{0,7},{9,8},{10,9},{11,1... | collective-permute-start | bytes 196616 | tf_op jit(solution)/shard_map/ppermute | solution.py:390
  41.0 2.7 %collective-permute-start.2 = (bf16[128,256]{1,0:T(8,128)(2,1)S(1)}, bf16[128,256]{1,0:T(8,128)(2,1)S(1)}, u32[]{:S(2)}, u32[]{:S(2)}) collective-permute-start(bf16[128,256]{1,0:T(8,128)(2,1)S(1)} %get-tuple-element.70), channel_id=1, source_target_pairs={{1,0},{2,1},{3,2},{4,3},{5,4},{6,5},{7,6},{0,7},{9,8},{10,9},{11,1... | collective-permute-start | bytes 196616 | tf_op jit(solution)/shard_map/ppermute | solution.py:390
  43.8 2.7 %collective-permute-start.14 = (bf16[256,256]{1,0:T(8,128)(2,1)S(1)}, bf16[256,256]{1,0:T(8,128)(2,1)S(1)}, u32[]{:S(2)}, u32[]{:S(2)}) collective-permute-start(bf16[256,256]{1,0:T(8,128)(2,1)S(1)} %get-tuple-element.91), channel_id=1, source_target_pairs={{1,0},{2,1},{3,2},{4,3},{5,4},{6,5},{7,6},{0,7},{9,8},{10,9},{11,1... | collective-permute-start | bytes 393224 | tf_op jit(solution)/shard_map/ppermute | solution.py:390
  46.6 2.7 %collective-permute-start.4 = (bf16[256,256]{1,0:T(8,128)(2,1)S(1)}, bf16[256,256]{1,0:T(8,128)(2,1)S(1)}, u32[]{:S(2)}, u32[]{:S(2)}) collective-permute-start(bf16[256,256]{1,0:T(8,128)(2,1)S(1)} %get-tuple-element.73), channel_id=1, source_target_pairs={{1,0},{2,1},{3,2},{4,3},{5,4},{6,5},{7,6},{0,7},{9,8},{10,9},{11,1... | collective-permute-start | bytes 393224 | tf_op jit(solution)/shard_map/ppermute | solution.py:390
  49.4 2.7 %collective-permute-start.16 = (bf16[256,256]{1,0:T(8,128)(2,1)S(1)}, bf16[256,256]{1,0:T(8,128)(2,1)S(1)}, u32[]{:S(2)}, u32[]{:S(2)}) collective-permute-start(bf16[256,256]{1,0:T(8,128)(2,1)S(1)} %get-tuple-element.94), channel_id=1, source_target_pairs={{1,0},{2,1},{3,2},{4,3},{5,4},{6,5},{7,6},{0,7},{9,8},{10,9},{11,1... | collective-permute-start | bytes 393224 | tf_op jit(solution)/shard_map/ppermute | solution.py:390
  52.7 2.5 %collective-permute-start.6 = (bf16[256,256]{1,0:T(8,128)(2,1)S(1)}, bf16[256,256]{1,0:T(8,128)(2,1)S(1)}, u32[]{:S(2)}, u32[]{:S(2)}) collective-permute-start(bf16[256,256]{1,0:T(8,128)(2,1)S(1)} %get-tuple-element.76), channel_id=1, source_target_pairs={{1,0},{2,1},{3,2},{4,3},{5,4},{6,5},{7,6},{0,7},{9,8},{10,9},{11,1... | collective-permute-start | bytes 393224 | tf_op jit(solution)/shard_map/ppermute | solution.py:390
  56.6 1.7 %collective-permute-start.18 = (bf16[256,256]{1,0:T(8,128)(2,1)S(1)}, bf16[256,256]{1,0:T(8,128)(2,1)S(1)}, u32[]{:S(2)}, u32[]{:S(2)}) collective-permute-start(bf16[256,256]{1,0:T(8,128)(2,1)S(1)} %get-tuple-element.96), channel_id=1, source_target_pairs={{1,0},{2,1},{3,2},{4,3},{5,4},{6,5},{7,6},{0,7},{9,8},{10,9},{11,1... | collective-permute-start | bytes 393224 | tf_op jit(solution)/shard_map/ppermute | solution.py:390
  59.0 3.1 %collective-permute-start.8 = (bf16[256,256]{1,0:T(8,128)(2,1)S(1)}, bf16[256,256]{1,0:T(8,128)(2,1)S(1)}, u32[]{:S(2)}, u32[]{:S(2)}) collective-permute-start(bf16[256,256]{1,0:T(8,128)(2,1)S(1)} %get-tuple-element.78), channel_id=1, source_target_pairs={{1,0},{2,1},{3,2},{4,3},{5,4},{6,5},{7,6},{0,7},{9,8},{10,9},{11,1... | collective-permute-start | bytes 393224 | tf_op jit(solution)/shard_map/ppermute | solution.py:390
  63.6 1.8 %collective-permute-done.7.first = bf16[256,256]{1,0:T(8,128)(2,1)S(1)} collective-permute-done((bf16[256,256]{1,0:T(8,128)(2,1)S(1)}, bf16[256,256]{1,0:T(8,128)(2,1)S(1)}, u32[]{:S(2)}, u32[]{:S(2)}) %collective-permute-start.7) | collective-permute-done | bytes 131104 | tf_op jit(solution)/shard_map/ppermute | solution.py:390
  65.5 2.2 %collective-permute-start.9 = (bf16[256,256]{1,0:T(8,128)(2,1)S(1)}, bf16[256,256]{1,0:T(8,128)(2,1)S(1)}, u32[]{:S(2)}, u32[]{:S(2)}) collective-permute-start(bf16[256,256]{1,0:T(8,128)(2,1)S(1)} %fold.2.own), channel_id=1, source_target_pairs={{0,8},{1,9},{2,10},{3,11},{4,12},{5,13},{6,14},{7,15},{8,0},{9,1},... | collective-permute-start | bytes 393224 | tf_op jit(solution)/shard_map/ppermute | solution.py:401
  68.3 2.4 %collective-permute-done.9.other = bf16[256,256]{1,0:T(8,128)(2,1)S(1)} collective-permute-done((bf16[256,256]{1,0:T(8,128)(2,1)S(1)}, bf16[256,256]{1,0:T(8,128)(2,1)S(1)}, u32[]{:S(2)}, u32[]{:S(2)}) %collective-permute-start.9) | collective-permute-done | bytes 131104 | tf_op jit(solution)/shard_map/ppermute | solution.py:401
  72.0 2.4 %collective-permute-start.21 = (bf16[512,256]{1,0:T(8,128)(2,1)S(1)}, bf16[512,256]{1,0:T(8,128)(2,1)S(1)}, u32[]{:S(2)}, u32[]{:S(2)}) collective-permute-start(bf16[512,256]{1,0:T(8,128)(2,1)S(1)} %get-tuple-element.111.refs_0_), channel_id=1, source_target_pairs={{1,0},{2,1},{3,2},{4,3},{5,4},{6,5},{7,6},{0,7},{9,8},{10,9},{11,1... | collective-permute-start | bytes 786440 | tf_op jit(solution)/shard_map/ppermute | solution.py:414
  74.4 3.3 %collective-permute-done.21.falling.refs_2_ = bf16[512,256]{1,0:T(8,128)(2,1)S(1)} collective-permute-done((bf16[512,256]{1,0:T(8,128)(2,1)S(1)}, bf16[512,256]{1,0:T(8,128)(2,1)S(1)}, u32[]{:S(2)}, u32[]{:S(2)}) %collective-permute-start.21) | collective-permute-done | bytes 262176 | tf_op jit(solution)/shard_map/ppermute | solution.py:414
  79.3 1.8 %collective-permute-start.23 = (bf16[544,256]{1,0:T(8,128)(2,1)S(1)}, bf16[544,256]{1,0:T(8,128)(2,1)S(1)}, u32[]{:S(2)}, u32[]{:S(2)}) collective-permute-start(bf16[544,256]{1,0:T(8,128)(2,1)S(1)} %get-tuple-element.105), channel_id=1, source_target_pairs={{1,0},{2,1},{3,2},{4,3},{5,4},{6,5},{7,6},{0,7},{9,8},{10,9},{11,1... | collective-permute-start | bytes 835592 | tf_op jit(solution)/shard_map/ppermute | solution.py:414
  81.1 5.9 %collective-permute-done.22.rising.refs_3_ = bf16[544,256]{1,0:T(8,128)(2,1)S(1)} collective-permute-done((bf16[544,256]{1,0:T(8,128)(2,1)S(1)}, bf16[544,256]{1,0:T(8,128)(2,1)S(1)}, u32[]{:S(2)}, u32[]{:S(2)}) %collective-permute-start.22) | collective-permute-done | bytes 278560 | tf_op jit(solution)/shard_map/ppermute | solution.py:413
  90.0 6.6 %collective-permute-done.24.rising.refs_5_ = bf16[544,256]{1,0:T(8,128)(2,1)S(1)} collective-permute-done((bf16[544,256]{1,0:T(8,128)(2,1)S(1)}, bf16[544,256]{1,0:T(8,128)(2,1)S(1)}, u32[]{:S(2)}, u32[]{:S(2)}) %collective-permute-start.24) | collective-permute-done | bytes 278560 | tf_op jit(solution)/shard_map/ppermute | solution.py:413
  97.5 1.9 %collective-permute-start.27 = (bf16[288,256]{1,0:T(8,128)(2,1)S(1)}, bf16[288,256]{1,0:T(8,128)(2,1)S(1)}, u32[]{:S(2)}, u32[]{:S(2)}) collective-permute-start(bf16[288,256]{1,0:T(8,128)(2,1)S(1)} %get-tuple-element.109), channel_id=1, source_target_pairs={{1,0},{2,1},{3,2},{4,3},{5,4},{6,5},{7,6},{0,7},{9,8},{10,9},{11,1... | collective-permute-start | bytes 442376 | tf_op jit(solution)/shard_map/ppermute | solution.py:421
  99.4 2.9 %collective-permute-done.26.rising.refs_7_ = bf16[288,256]{1,0:T(8,128)(2,1)S(1)} collective-permute-done((bf16[288,256]{1,0:T(8,128)(2,1)S(1)}, bf16[288,256]{1,0:T(8,128)(2,1)S(1)}, u32[]{:S(2)}, u32[]{:S(2)}) %collective-permute-start.26) | collective-permute-done | bytes 147488 | tf_op jit(solution)/shard_map/ppermute | solution.py:420
  103.0 3.4 %all-to-all-start.1 = ((bf16[8,32,256]{2,1,0:T(8,128)(2,1)}), bf16[8,32,256]{2,1,0:T(8,128)(2,1)S(1)}, u32[]{:S(2)}, u32[]{:S(2)}) async-start(bf16[8,32,256]{2,1,0:T(8,128)(2,1)} %ring_sum.1), calls=%async_computation.1 | async-start | bytes 262144 | tf_op jit(solution)/shard_map/all_to_all | solution.py:369
  106.4 5.1 %spmm_back.1 = (bf16[2048,256]{1,0:T(8,128)(2,1)S(1)}, bf16[2048,256]{1,0:T(8,128)(2,1)S(1)}) custom-call(s32[1]{0:T(128)} %bitcast.12.live, s32[160]{0:T(256)S(1)} %get-tuple-element.129.src.dst, s32[160]{0:T(256)S(1)} %get-tuple-element.125.src, bf16[512,256]{1,0:T(8,128)(2,1)S(1)} %get-tuple-element.111.refs_0_, ...), custom_call_target="tpu_custom_call" | custom-call | flops 13421772800 | bytes 37748736 | tf_op jit(solution)/shard_map/spmm_back/pallas_call | solution.py:88
  113.4 11.1 %collective-permute-start.36 = (bf16[2048,256]{1,0:T(8,128)(2,1)}, bf16[2048,256]{1,0:T(8,128)(2,1)S(1)}, u32[]{:S(2)}, u32[]{:S(2)}) collective-permute-start(bf16[2048,256]{1,0:T(8,128)(2,1)} %copy-done.2), channel_id=1, source_target_pairs={{0,16},{16,0},{32,48},{48,32},{64,80},{80,64},{96,112},{112,96},{1... | collective-permute-start | bytes 3145736 | tf_op jit(solution)/shard_map/ppermute | solution.py:433
  124.5 2.5 %collective-permute-done.36.second = bf16[2048,256]{1,0:T(8,128)(2,1)S(1)} collective-permute-done((bf16[2048,256]{1,0:T(8,128)(2,1)}, bf16[2048,256]{1,0:T(8,128)(2,1)S(1)}, u32[]{:S(2)}, u32[]{:S(2)}) %collective-permute-start.36) | collective-permute-done | bytes 1048608 | tf_op jit(solution)/shard_map/ppermute | solution.py:433
  128.3 4.9 %all-to-all-start.2 = ((bf16[8,256,256]{2,1,0:T(8,128)(2,1)}), bf16[8,256,256]{2,1,0:T(8,128)(2,1)S(1)}, u32[]{:S(2)}, u32[]{:S(2)}) async-start(bf16[8,256,256]{2,1,0:T(8,128)(2,1)} %bitcast.9), calls=%async_computation.2 | async-start | bytes 2097152 | tf_op jit(solution)/shard_map/all_to_all | solution.py:369
  136.1 2.7 %collective-permute-start.34 = (f32[32,256]{1,0:T(8,128)S(1)}, f32[32,256]{1,0:T(8,128)S(1)}, u32[]{:S(2)}, u32[]{:S(2)}) collective-permute-start(f32[32,256]{1,0:T(8,128)S(1)} %add.119.refs_0_), channel_id=1, source_target_pairs={{0,2},{1,3},{2,4},{3,5},{4,6},{5,7},{6,0},{7,1},{8,10},{9,11},{10,... | collective-permute-start | bytes 98312 | tf_op jit(solution)/shard_map/ppermute | solution.py:439
  138.8 2.0 %collective-permute-start.33 = (f32[32,256]{1,0:T(8,128)S(1)}, f32[32,256]{1,0:T(8,128)S(1)}, u32[]{:S(2)}, u32[]{:S(2)}) collective-permute-start(f32[32,256]{1,0:T(8,128)S(1)} %add.119.refs_0_), channel_id=1, source_target_pairs={{0,3},{1,4},{2,5},{3,6},{4,7},{5,0},{6,1},{7,2},{8,11},{9,12},{10,... | collective-permute-start | bytes 98312 | tf_op jit(solution)/shard_map/ppermute | solution.py:439
  140.8 2.0 %collective-permute-start.32 = (f32[32,256]{1,0:T(8,128)S(1)}, f32[32,256]{1,0:T(8,128)S(1)}, u32[]{:S(2)}, u32[]{:S(2)}) collective-permute-start(f32[32,256]{1,0:T(8,128)S(1)} %add.119.refs_0_), channel_id=1, source_target_pairs={{0,4},{1,5},{2,6},{3,7},{4,0},{5,1},{6,2},{7,3},{8,12},{9,13},{10,... | collective-permute-start | bytes 98312 | tf_op jit(solution)/shard_map/ppermute | solution.py:439
  142.8 2.5 %collective-permute-start.31 = (f32[32,256]{1,0:T(8,128)S(1)}, f32[32,256]{1,0:T(8,128)S(1)}, u32[]{:S(2)}, u32[]{:S(2)}) collective-permute-start(f32[32,256]{1,0:T(8,128)S(1)} %add.119.refs_0_), channel_id=1, source_target_pairs={{0,5},{1,6},{2,7},{3,0},{4,1},{5,2},{6,3},{7,4},{8,13},{9,14},{10,... | collective-permute-start | bytes 98312 | tf_op jit(solution)/shard_map/ppermute | solution.py:439
  145.3 1.7 %collective-permute-start.30 = (f32[32,256]{1,0:T(8,128)S(1)}, f32[32,256]{1,0:T(8,128)S(1)}, u32[]{:S(2)}, u32[]{:S(2)}) collective-permute-start(f32[32,256]{1,0:T(8,128)S(1)} %add.119.refs_0_), channel_id=1, source_target_pairs={{0,6},{1,7},{2,0},{3,1},{4,2},{5,3},{6,4},{7,5},{8,14},{9,15},{10,... | collective-permute-start | bytes 98312 | tf_op jit(solution)/shard_map/ppermute | solution.py:439
  148.0 2.4 %collective-permute-done.30.refs_2_ = f32[32,256]{1,0:T(8,128)S(1)} collective-permute-done((f32[32,256]{1,0:T(8,128)S(1)}, f32[32,256]{1,0:T(8,128)S(1)}, u32[]{:S(2)}, u32[]{:S(2)}) %collective-permute-start.30) | collective-permute-done | bytes 32800 | tf_op jit(solution)/shard_map/ppermute | solution.py:439
  (77 shorter events, 25.5 us)
Async XLA Ops:
  27.0 16.6 %collective-permute-start.12 = (bf16[256,256]{1,0:T(8,128)(2,1)}, bf16[256,256]{1,0:T(8,128)(2,1)S(1)}, u32[]{:S(2)}, u32[]{:S(2)}) collective-permute-start(bf16[256,256]{1,0:T(8,128)(2,1)} %bitcast.15), channel_id=1, source_target_pairs={{0,8},{1,9},{2,10},{3,11},{4,12},{5,13},{6,14},{7,15},{8,0},{9,1},... | collective-permute-start | bytes 393224 | tf_op jit(solution)/shard_map/ppermute | solution.py:386
  34.5 9.1 %collective-permute-start.10 = (bf16[128,256]{1,0:T(8,128)(2,1)S(1)}, bf16[128,256]{1,0:T(8,128)(2,1)S(1)}, u32[]{:S(2)}, u32[]{:S(2)}) collective-permute-start(bf16[128,256]{1,0:T(8,128)(2,1)S(1)} %get-tuple-element.79), channel_id=1, source_target_pairs={{0,1},{1,2},{2,3},{3,4},{4,5},{5,6},{6,7},{7,0},{8,9},{9,10},{10,1... | collective-permute-start | bytes 196616 | tf_op jit(solution)/shard_map/ppermute | solution.py:390
  35.5 8.1 %collective-permute-start.11 = (bf16[128,256]{1,0:T(8,128)(2,1)S(1)}, bf16[128,256]{1,0:T(8,128)(2,1)S(1)}, u32[]{:S(2)}, u32[]{:S(2)}) collective-permute-start(bf16[128,256]{1,0:T(8,128)(2,1)S(1)} %get-tuple-element.80), channel_id=1, source_target_pairs={{1,0},{2,1},{3,2},{4,3},{5,4},{6,5},{7,6},{0,7},{9,8},{10,9},{11,1... | collective-permute-start | bytes 196616 | tf_op jit(solution)/shard_map/ppermute | solution.py:390
  41.0 5.5 %collective-permute-start.1 = (bf16[128,256]{1,0:T(8,128)(2,1)S(1)}, bf16[128,256]{1,0:T(8,128)(2,1)S(1)}, u32[]{:S(2)}, u32[]{:S(2)}) collective-permute-start(bf16[128,256]{1,0:T(8,128)(2,1)S(1)} %get-tuple-element.68), channel_id=1, source_target_pairs={{0,1},{1,2},{2,3},{3,4},{4,5},{5,6},{6,7},{7,0},{8,9},{9,10},{10,1... | collective-permute-start | bytes 196616 | tf_op jit(solution)/shard_map/ppermute | solution.py:390
  41.0 5.5 %collective-permute-start.2 = (bf16[128,256]{1,0:T(8,128)(2,1)S(1)}, bf16[128,256]{1,0:T(8,128)(2,1)S(1)}, u32[]{:S(2)}, u32[]{:S(2)}) collective-permute-start(bf16[128,256]{1,0:T(8,128)(2,1)S(1)} %get-tuple-element.70), channel_id=1, source_target_pairs={{1,0},{2,1},{3,2},{4,3},{5,4},{6,5},{7,6},{0,7},{9,8},{10,9},{11,1... | collective-permute-start | bytes 196616 | tf_op jit(solution)/shard_map/ppermute | solution.py:390
  43.7 5.6 %collective-permute-start.13 = (bf16[256,256]{1,0:T(8,128)(2,1)S(1)}, bf16[256,256]{1,0:T(8,128)(2,1)S(1)}, u32[]{:S(2)}, u32[]{:S(2)}) collective-permute-start(bf16[256,256]{1,0:T(8,128)(2,1)S(1)} %get-tuple-element.89), channel_id=1, source_target_pairs={{0,1},{1,2},{2,3},{3,4},{4,5},{5,6},{6,7},{7,0},{8,9},{9,10},{10,1... | collective-permute-start | bytes 393224 | tf_op jit(solution)/shard_map/ppermute | solution.py:390
  43.8 5.5 %collective-permute-start.14 = (bf16[256,256]{1,0:T(8,128)(2,1)S(1)}, bf16[256,256]{1,0:T(8,128)(2,1)S(1)}, u32[]{:S(2)}, u32[]{:S(2)}) collective-permute-start(bf16[256,256]{1,0:T(8,128)(2,1)S(1)} %get-tuple-element.91), channel_id=1, source_target_pairs={{1,0},{2,1},{3,2},{4,3},{5,4},{6,5},{7,6},{0,7},{9,8},{10,9},{11,1... | collective-permute-start | bytes 393224 | tf_op jit(solution)/shard_map/ppermute | solution.py:390
  46.5 5.6 %collective-permute-start.3 = (bf16[256,256]{1,0:T(8,128)(2,1)S(1)}, bf16[256,256]{1,0:T(8,128)(2,1)S(1)}, u32[]{:S(2)}, u32[]{:S(2)}) collective-permute-start(bf16[256,256]{1,0:T(8,128)(2,1)S(1)} %get-tuple-element.71), channel_id=1, source_target_pairs={{0,1},{1,2},{2,3},{3,4},{4,5},{5,6},{6,7},{7,0},{8,9},{9,10},{10,1... | collective-permute-start | bytes 393224 | tf_op jit(solution)/shard_map/ppermute | solution.py:390
  46.6 5.5 %collective-permute-start.4 = (bf16[256,256]{1,0:T(8,128)(2,1)S(1)}, bf16[256,256]{1,0:T(8,128)(2,1)S(1)}, u32[]{:S(2)}, u32[]{:S(2)}) collective-permute-start(bf16[256,256]{1,0:T(8,128)(2,1)S(1)} %get-tuple-element.73), channel_id=1, source_target_pairs={{1,0},{2,1},{3,2},{4,3},{5,4},{6,5},{7,6},{0,7},{9,8},{10,9},{11,1... | collective-permute-start | bytes 393224 | tf_op jit(solution)/shard_map/ppermute | solution.py:390
  49.3 5.8 %collective-permute-start.15 = (bf16[256,256]{1,0:T(8,128)(2,1)S(1)}, bf16[256,256]{1,0:T(8,128)(2,1)S(1)}, u32[]{:S(2)}, u32[]{:S(2)}) collective-permute-start(bf16[256,256]{1,0:T(8,128)(2,1)S(1)} %get-tuple-element.92), channel_id=1, source_target_pairs={{0,1},{1,2},{2,3},{3,4},{4,5},{5,6},{6,7},{7,0},{8,9},{9,10},{10,1... | collective-permute-start | bytes 393224 | tf_op jit(solution)/shard_map/ppermute | solution.py:390
  49.4 5.8 %collective-permute-start.16 = (bf16[256,256]{1,0:T(8,128)(2,1)S(1)}, bf16[256,256]{1,0:T(8,128)(2,1)S(1)}, u32[]{:S(2)}, u32[]{:S(2)}) collective-permute-start(bf16[256,256]{1,0:T(8,128)(2,1)S(1)} %get-tuple-element.94), channel_id=1, source_target_pairs={{1,0},{2,1},{3,2},{4,3},{5,4},{6,5},{7,6},{0,7},{9,8},{10,9},{11,1... | collective-permute-start | bytes 393224 | tf_op jit(solution)/shard_map/ppermute | solution.py:390
  52.2 6.7 %collective-permute-start.5 = (bf16[256,256]{1,0:T(8,128)(2,1)S(1)}, bf16[256,256]{1,0:T(8,128)(2,1)S(1)}, u32[]{:S(2)}, u32[]{:S(2)}) collective-permute-start(bf16[256,256]{1,0:T(8,128)(2,1)S(1)} %get-tuple-element.74), channel_id=1, source_target_pairs={{0,1},{1,2},{2,3},{3,4},{4,5},{5,6},{6,7},{7,0},{8,9},{9,10},{10,1... | collective-permute-start | bytes 393224 | tf_op jit(solution)/shard_map/ppermute | solution.py:390
  52.7 6.2 %collective-permute-start.6 = (bf16[256,256]{1,0:T(8,128)(2,1)S(1)}, bf16[256,256]{1,0:T(8,128)(2,1)S(1)}, u32[]{:S(2)}, u32[]{:S(2)}) collective-permute-start(bf16[256,256]{1,0:T(8,128)(2,1)S(1)} %get-tuple-element.76), channel_id=1, source_target_pairs={{1,0},{2,1},{3,2},{4,3},{5,4},{6,5},{7,6},{0,7},{9,8},{10,9},{11,1... | collective-permute-start | bytes 393224 | tf_op jit(solution)/shard_map/ppermute | solution.py:390
  55.2 6.8 %collective-permute-start.17 = (bf16[256,256]{1,0:T(8,128)(2,1)S(1)}, bf16[256,256]{1,0:T(8,128)(2,1)S(1)}, u32[]{:S(2)}, u32[]{:S(2)}) collective-permute-start(bf16[256,256]{1,0:T(8,128)(2,1)S(1)} %get-tuple-element.95), channel_id=1, source_target_pairs={{0,1},{1,2},{2,3},{3,4},{4,5},{5,6},{6,7},{7,0},{8,9},{9,10},{10,1... | collective-permute-start | bytes 393224 | tf_op jit(solution)/shard_map/ppermute | solution.py:390
  56.6 5.5 %collective-permute-start.18 = (bf16[256,256]{1,0:T(8,128)(2,1)S(1)}, bf16[256,256]{1,0:T(8,128)(2,1)S(1)}, u32[]{:S(2)}, u32[]{:S(2)}) collective-permute-start(bf16[256,256]{1,0:T(8,128)(2,1)S(1)} %get-tuple-element.96), channel_id=1, source_target_pairs={{1,0},{2,1},{3,2},{4,3},{5,4},{6,5},{7,6},{0,7},{9,8},{10,9},{11,1... | collective-permute-start | bytes 393224 | tf_op jit(solution)/shard_map/ppermute | solution.py:390
  58.9 6.6 %collective-permute-start.7 = (bf16[256,256]{1,0:T(8,128)(2,1)S(1)}, bf16[256,256]{1,0:T(8,128)(2,1)S(1)}, u32[]{:S(2)}, u32[]{:S(2)}) collective-permute-start(bf16[256,256]{1,0:T(8,128)(2,1)S(1)} %get-tuple-element.77), channel_id=1, source_target_pairs={{0,1},{1,2},{2,3},{3,4},{4,5},{5,6},{6,7},{7,0},{8,9},{9,10},{10,1... | collective-permute-start | bytes 393224 | tf_op jit(solution)/shard_map/ppermute | solution.py:390
  59.0 6.5 %collective-permute-start.8 = (bf16[256,256]{1,0:T(8,128)(2,1)S(1)}, bf16[256,256]{1,0:T(8,128)(2,1)S(1)}, u32[]{:S(2)}, u32[]{:S(2)}) collective-permute-start(bf16[256,256]{1,0:T(8,128)(2,1)S(1)} %get-tuple-element.78), channel_id=1, source_target_pairs={{1,0},{2,1},{3,2},{4,3},{5,4},{6,5},{7,6},{0,7},{9,8},{10,9},{11,1... | collective-permute-start | bytes 393224 | tf_op jit(solution)/shard_map/ppermute | solution.py:390
  62.1 5.6 %collective-permute-start.19 = (bf16[256,256]{1,0:T(8,128)(2,1)S(1)}, bf16[256,256]{1,0:T(8,128)(2,1)S(1)}, u32[]{:S(2)}, u32[]{:S(2)}) collective-permute-start(bf16[256,256]{1,0:T(8,128)(2,1)S(1)} %fold.3.own), channel_id=1, source_target_pairs={{0,8},{1,9},{2,10},{3,11},{4,12},{5,13},{6,14},{7,15},{8,0},{9,1},... | collective-permute-start | bytes 393224 | tf_op jit(solution)/shard_map/ppermute | solution.py:401
  71.7 6.6 %collective-permute-start.20 = (bf16[544,256]{1,0:T(8,128)(2,1)S(1)}, bf16[544,256]{1,0:T(8,128)(2,1)S(1)}, u32[]{:S(2)}, u32[]{:S(2)}) collective-permute-start(bf16[544,256]{1,0:T(8,128)(2,1)S(1)} %get-tuple-element.101), channel_id=1, source_target_pairs={{0,1},{1,2},{2,3},{3,4},{4,5},{5,6},{6,7},{7,0},{8,9},{9,10},{10,1... | collective-permute-start | bytes 835592 | tf_op jit(solution)/shard_map/ppermute | solution.py:413
  72.0 5.7 %collective-permute-start.21 = (bf16[512,256]{1,0:T(8,128)(2,1)S(1)}, bf16[512,256]{1,0:T(8,128)(2,1)S(1)}, u32[]{:S(2)}, u32[]{:S(2)}) collective-permute-start(bf16[512,256]{1,0:T(8,128)(2,1)S(1)} %get-tuple-element.111.refs_0_), channel_id=1, source_target_pairs={{1,0},{2,1},{3,2},{4,3},{5,4},{6,5},{7,6},{0,7},{9,8},{10,9},{11,1... | collective-permute-start | bytes 786440 | tf_op jit(solution)/shard_map/ppermute | solution.py:414
  78.3 8.7 %collective-permute-start.22 = (bf16[544,256]{1,0:T(8,128)(2,1)S(1)}, bf16[544,256]{1,0:T(8,128)(2,1)S(1)}, u32[]{:S(2)}, u32[]{:S(2)}) collective-permute-start(bf16[544,256]{1,0:T(8,128)(2,1)S(1)} %get-tuple-element.104), channel_id=1, source_target_pairs={{0,1},{1,2},{2,3},{3,4},{4,5},{5,6},{6,7},{7,0},{8,9},{9,10},{10,1... | collective-permute-start | bytes 835592 | tf_op jit(solution)/shard_map/ppermute | solution.py:413
  79.3 7.9 %collective-permute-start.23 = (bf16[544,256]{1,0:T(8,128)(2,1)S(1)}, bf16[544,256]{1,0:T(8,128)(2,1)S(1)}, u32[]{:S(2)}, u32[]{:S(2)}) collective-permute-start(bf16[544,256]{1,0:T(8,128)(2,1)S(1)} %get-tuple-element.105), channel_id=1, source_target_pairs={{1,0},{2,1},{3,2},{4,3},{5,4},{6,5},{7,6},{0,7},{9,8},{10,9},{11,1... | collective-permute-start | bytes 835592 | tf_op jit(solution)/shard_map/ppermute | solution.py:414
  87.2 9.4 %collective-permute-start.24 = (bf16[544,256]{1,0:T(8,128)(2,1)S(1)}, bf16[544,256]{1,0:T(8,128)(2,1)S(1)}, u32[]{:S(2)}, u32[]{:S(2)}) collective-permute-start(bf16[544,256]{1,0:T(8,128)(2,1)S(1)} %get-tuple-element.106), channel_id=1, source_target_pairs={{0,1},{1,2},{2,3},{3,4},{4,5},{5,6},{6,7},{7,0},{8,9},{9,10},{10,1... | collective-permute-start | bytes 835592 | tf_op jit(solution)/shard_map/ppermute | solution.py:413
  88.4 8.2 %collective-permute-start.25 = (bf16[544,256]{1,0:T(8,128)(2,1)S(1)}, bf16[544,256]{1,0:T(8,128)(2,1)S(1)}, u32[]{:S(2)}, u32[]{:S(2)}) collective-permute-start(bf16[544,256]{1,0:T(8,128)(2,1)S(1)} %get-tuple-element.107), channel_id=1, source_target_pairs={{1,0},{2,1},{3,2},{4,3},{5,4},{6,5},{7,6},{0,7},{9,8},{10,9},{11,1... | collective-permute-start | bytes 835592 | tf_op jit(solution)/shard_map/ppermute | solution.py:414
  96.6 5.6 %collective-permute-start.26 = (bf16[288,256]{1,0:T(8,128)(2,1)S(1)}, bf16[288,256]{1,0:T(8,128)(2,1)S(1)}, u32[]{:S(2)}, u32[]{:S(2)}) collective-permute-start(bf16[288,256]{1,0:T(8,128)(2,1)S(1)} %get-tuple-element.108), channel_id=1, source_target_pairs={{0,1},{1,2},{2,3},{3,4},{4,5},{5,6},{6,7},{7,0},{8,9},{9,10},{10,1... | collective-permute-start | bytes 442376 | tf_op jit(solution)/shard_map/ppermute | solution.py:420
  103.0 10.4 %all-to-all-start.1 = ((bf16[8,32,256]{2,1,0:T(8,128)(2,1)}), bf16[8,32,256]{2,1,0:T(8,128)(2,1)S(1)}, u32[]{:S(2)}, u32[]{:S(2)}) async-start(bf16[8,32,256]{2,1,0:T(8,128)(2,1)} %ring_sum.1), calls=%async_computation.1 | async-start | bytes 262144 | tf_op jit(solution)/shard_map/all_to_all | solution.py:369
  113.4 13.6 %collective-permute-start.36 = (bf16[2048,256]{1,0:T(8,128)(2,1)}, bf16[2048,256]{1,0:T(8,128)(2,1)S(1)}, u32[]{:S(2)}, u32[]{:S(2)}) collective-permute-start(bf16[2048,256]{1,0:T(8,128)(2,1)} %copy-done.2), channel_id=1, source_target_pairs={{0,16},{16,0},{32,48},{48,32},{64,80},{80,64},{96,112},{112,96},{1... | collective-permute-start | bytes 3145736 | tf_op jit(solution)/shard_map/ppermute | solution.py:433
  128.3 23.3 %all-to-all-start.2 = ((bf16[8,256,256]{2,1,0:T(8,128)(2,1)}), bf16[8,256,256]{2,1,0:T(8,128)(2,1)S(1)}, u32[]{:S(2)}, u32[]{:S(2)}) async-start(bf16[8,256,256]{2,1,0:T(8,128)(2,1)} %bitcast.9), calls=%async_computation.2 | async-start | bytes 2097152 | tf_op jit(solution)/shard_map/all_to_all | solution.py:369
  134.7 10.6 %collective-permute-start.35 = (f32[32,256]{1,0:T(8,128)S(1)}, f32[32,256]{1,0:T(8,128)S(1)}, u32[]{:S(2)}, u32[]{:S(2)}) collective-permute-start(f32[32,256]{1,0:T(8,128)S(1)} %add.119.refs_0_), channel_id=1, source_target_pairs={{0,1},{1,2},{2,3},{3,4},{4,5},{5,6},{6,7},{7,0},{8,9},{9,10},{10,1... | collective-permute-start | bytes 98312 | tf_op jit(solution)/shard_map/ppermute | solution.py:439
  136.1 10.8 %collective-permute-start.34 = (f32[32,256]{1,0:T(8,128)S(1)}, f32[32,256]{1,0:T(8,128)S(1)}, u32[]{:S(2)}, u32[]{:S(2)}) collective-permute-start(f32[32,256]{1,0:T(8,128)S(1)} %add.119.refs_0_), channel_id=1, source_target_pairs={{0,2},{1,3},{2,4},{3,5},{4,6},{5,7},{6,0},{7,1},{8,10},{9,11},{10,... | collective-permute-start | bytes 98312 | tf_op jit(solution)/shard_map/ppermute | solution.py:439
  138.8 9.1 %collective-permute-start.33 = (f32[32,256]{1,0:T(8,128)S(1)}, f32[32,256]{1,0:T(8,128)S(1)}, u32[]{:S(2)}, u32[]{:S(2)}) collective-permute-start(f32[32,256]{1,0:T(8,128)S(1)} %add.119.refs_0_), channel_id=1, source_target_pairs={{0,3},{1,4},{2,5},{3,6},{4,7},{5,0},{6,1},{7,2},{8,11},{9,12},{10,... | collective-permute-start | bytes 98312 | tf_op jit(solution)/shard_map/ppermute | solution.py:439
  140.8 7.1 %collective-permute-start.32 = (f32[32,256]{1,0:T(8,128)S(1)}, f32[32,256]{1,0:T(8,128)S(1)}, u32[]{:S(2)}, u32[]{:S(2)}) collective-permute-start(f32[32,256]{1,0:T(8,128)S(1)} %add.119.refs_0_), channel_id=1, source_target_pairs={{0,4},{1,5},{2,6},{3,7},{4,0},{5,1},{6,2},{7,3},{8,12},{9,13},{10,... | collective-permute-start | bytes 98312 | tf_op jit(solution)/shard_map/ppermute | solution.py:439
  (10 other events, 107.6 us)
